TPU v7x, 256 devices: a whole 4x4x8 slice. The times are simulated.
256 devices in a mesh: grp: 64 (over x, z, core), slab: 4 (over y).
Axes of the slice: x: 4, y: 4, z: 8, core: 2. Of those that a mesh axis runs over, the one named last changes fastest.
Arguments:
- support: bfloat16 [1024, 32, 32, 128], P('grp', None, 'slab'), may hold values from -6 to 6
- corners: int32 [1024], P('grp'), may hold values from 0 to 2047, as said below
- occupation: bfloat16 [1024], P('grp'), may hold values from 0.019897461 to 0.099609375
- potential: float32 [2048, 32, 128], P('grp', 'slab'), may hold values from -4 to 4
Outputs:
- applied: bfloat16 [1024, 32, 32, 128], P('grp', None, 'slab')
- density: float32 [2048, 32, 128], P('grp', 'slab')
Inputs may be any that keep to these rules, and one draw needn't show every extreme that they name: corners[k] starts a region of 32 consecutive y planes counted modulo 2048. All regions of one group (the 16 consecutive functions held by one grp index) start at the same offset modulo 32. Of one group's region planes at most 32 lie in one block of planes b*32 to b*32 + 31, and in every draw some block receives exactly 32 from every group.
All inputs are finite; a program needn't handle non-finite values.
Results may differ from a plain program's by a relative error of at most 0.0045.
Values may be sent and summed in bfloat16 or wider, within the bound.
A program may use at most 192 MiB of HBM per device.

v0:
```python
import math

import jax
import jax.numpy as jnp
from jax import lax
from jax.sharding import PartitionSpec as P

kinetic_taps = [
    2.0 * (-1.0) ** (index + 2) / float((index + 1) * (index + 1)) for index in range(8)
]
center_tap = -math.pi * math.pi / 3.0


def with_halo(cells, sides, width):
    for axis, dim in sides:
        count = lax.axis_size(axis)
        head = lax.slice_in_dim(cells, 0, width, axis=dim)
        tail = lax.slice_in_dim(cells, cells.shape[dim] - width, cells.shape[dim], axis=dim)
        cells = jnp.concatenate(
            [
                lax.ppermute(tail, axis, [(i, (i + 1) % count) for i in range(count)]),
                cells,
                lax.ppermute(head, axis, [((i + 1) % count, i) for i in range(count)]),
            ],
            axis=dim,
        )
    return cells


def laplace_local(extended, values):
    x_cells = values.shape[2]
    wide = extended.astype(jnp.float32)
    total = 3.0 * center_tap * values
    padded = jnp.pad(values, ((0, 0), (8, 8), (0, 0), (0, 0)))
    planes = values.shape[1]
    for offset in range(1, 9):
        weight = kinetic_taps[offset - 1]
        along_y = (
            padded[:, 8 + offset : 8 + offset + planes]
            + padded[:, 8 - offset : 8 - offset + planes]
        )
        along_x = (
            wide[:, :, 8 + offset : 8 + offset + x_cells]
            + wide[:, :, 8 - offset : 8 - offset + x_cells]
        )
        along_z = jnp.roll(values, offset, 3) + jnp.roll(values, -offset, 3)
        total = total + weight * (along_y + along_x + along_z)
    return total


def on_device(support, corners, occupation, potential):
    sf_count, box_rows, x_cells, z_cells = support.shape
    cells = x_cells * z_cells
    groups = lax.axis_size("grp")
    planes_all = groups * box_rows
    extended = with_halo(support, (("slab", 2),), 8)
    values = support.astype(jnp.float32)
    laplace_term = laplace_local(extended, values)
    plane = (
        (corners[:, None] + jnp.arange(box_rows, dtype=jnp.int32)[None, :]) % planes_all
    ).reshape(-1)
    rows_float = values.reshape(sf_count * box_rows, cells)
    row_weights = jnp.repeat(occupation, box_rows)
    whole = (
        lax.all_gather(potential.astype(jnp.bfloat16), "grp", axis=0, tiled=True)
        .astype(potential.dtype)
        .reshape(planes_all, cells)
    )
    potential_term = (jnp.take(whole, plane, axis=0) * rows_float).astype(jnp.bfloat16)
    potential_term = lax.optimization_barrier(potential_term)
    terms = row_weights.astype(jnp.float32)[:, None] * rows_float * rows_float
    partial_value = jnp.zeros((planes_all, cells), jnp.float32).at[plane].add(terms)
    density = lax.psum_scatter(partial_value, "grp", scatter_dimension=0, tiled=True)
    applied = (
        -0.5 * laplace_term
        + potential_term.reshape(sf_count, box_rows, x_cells, z_cells).astype(jnp.float32)
    ).astype(jnp.bfloat16)
    return (applied, density.reshape(box_rows, x_cells, z_cells))


def solution(mesh):
    in_specs = (P("grp", None, "slab", None), P("grp"), P("grp"), P("grp", "slab", None))
    out_specs = (P("grp", None, "slab", None), P("grp", "slab", None))
    return jax.shard_map(
        on_device, mesh=mesh, in_specs=in_specs, out_specs=out_specs, check_vma=False
    )
```

profile of v0, /device:TPU:1, one launch (start us, length us, event | category | flops | bytes accessed | tf_op | source)
XLA Modules:
  0.0 250.9 jit_solution(4699402536544148141)
XLA Ops:
  7.2 1.5 convert_element_type.37
  10.4 1.4 convert_element_type.35
  11.9 8.8 %scatter_custom_fusion = f32[2048,1024]{1,0:T(8,128)} fusion(s32[512]{0:T(512)S(1)} %bitcast.33, f32[]{:T(128)} %constant.21.clone.1, f32[64,8,8,128]{3,2,1,0:T(8,128)S(1)} %bitcast.27, f32[512]{0:T(512)S(1)} %convert_element_type.43), kind=kCustom, calls=%fused_computation.19 | custom fusion | flops 1572864 | bytes 10487812 | tf_op jit(solution)/shard_map/scatter-add | solution.py:72
  20.7 1.2 copy-done
  21.9 2.1 collective-permute-start
  24.0 1.4 collective-permute-start.1
  25.6 2.6 %fusion.59 = (f32[16,32,8,5]{3,2,1,0:T(8,128)}, f32[16,32,8,5]{3,2,1,0:T(8,128)}) fusion(bf16[16,32,8,128]{3,2,1,0:T(8,128)(2,1)S(1)} %copy-done), kind=kLoop, calls=%fused_computation.109 | loop fusion | bytes 327680 | tf_op jit(solution)/shard_map/jit(_roll_static)/slice | solution.py:46
  28.1 2.5 fusion.60
  30.6 2.5 fusion.57
  33.1 2.5 %fusion.58 = (f32[16,32,8,124]{3,2,1,0:T(8,128)}, f32[16,32,8,124]{3,2,1,0:T(8,128)}) fusion(bf16[16,32,8,128]{3,2,1,0:T(8,128)(2,1)S(1)} %copy-done), kind=kLoop, calls=%fused_computation.108 | loop fusion | bytes 8126464 | tf_op jit(solution)/shard_map/jit(_roll_static)/slice | solution.py:46
  35.6 2.4 fusion.61
  38.1 2.6 %fusion.62 = (f32[16,32,8,122]{3,2,1,0:T(8,128)}, f32[16,32,8,122]{3,2,1,0:T(8,128)}) fusion(bf16[16,32,8,128]{3,2,1,0:T(8,128)(2,1)S(1)} %copy-done), kind=kLoop, calls=%fused_computation.112 | loop fusion | bytes 7995392 | tf_op jit(solution)/shard_map/jit(_roll_static)/slice | solution.py:46
  40.7 2.6 %fusion.54 = (f32[16,32,8,126]{3,2,1,0:T(8,128)}, f32[16,32,8,126]{3,2,1,0:T(8,128)}) fusion(bf16[16,32,8,128]{3,2,1,0:T(8,128)(2,1)S(1)} %copy-done), kind=kLoop, calls=%fused_computation.104 | loop fusion | bytes 8257536 | tf_op jit(solution)/shard_map/jit(_roll_static)/slice | solution.py:46
  43.3 2.5 fusion.53
  45.7 2.5 fusion.63
  48.2 2.5 %fusion.64 = (f32[16,32,8,121]{3,2,1,0:T(8,128)}, f32[16,32,8,121]{3,2,1,0:T(8,128)}) fusion(bf16[16,32,8,128]{3,2,1,0:T(8,128)(2,1)S(1)} %copy-done), kind=kLoop, calls=%fused_computation.114 | loop fusion | bytes 7929856 | tf_op jit(solution)/shard_map/jit(_roll_static)/slice | solution.py:46
  50.8 2.5 fusion.56
  53.3 2.5 fusion.55
  55.7 2.4 fusion.65
  58.2 2.6 %fusion.66 = (f32[16,32,8,120]{3,2,1,0:T(8,128)}, f32[16,32,8,120]{3,2,1,0:T(8,128)}) fusion(bf16[16,32,8,128]{3,2,1,0:T(8,128)(2,1)S(1)} %copy-done), kind=kLoop, calls=%fused_computation.116 | loop fusion | bytes 7864320 | tf_op jit(solution)/shard_map/jit(_roll_static)/slice | solution.py:46
  60.7 2.5 fusion.52
  63.2 2.5 %fusion.51 = (f32[16,32,8,1]{3,2,1,0:T(8,128)}, f32[16,32,8,1]{3,2,1,0:T(8,128)}) fusion(bf16[16,32,8,128]{3,2,1,0:T(8,128)(2,1)S(1)} %copy-done), kind=kLoop, calls=%fused_computation.101 | loop fusion | bytes 65536 | tf_op jit(solution)/shard_map/jit(_roll_static)/slice | solution.py:46
  65.7 4.6 %maximum_convert_fusion = f32[16,32,24,128]{3,2,1,0:T(8,128)} fusion(bf16[16,32,8,128]{3,2,1,0:T(8,128)(2,1)} %collective-permute-done.1, bf16[16,32,8,128]{3,2,1,0:T(8,128)(2,1)S(1)} %copy-done, bf16[16,32,8,128]{3,2,1,0:T(8,128)(2,1)} %collective-permute-done), kind=kLoop, calls=%fused_computation.21 | loop fusion | flops 9437184 | bytes 9437184 | tf_op jit(solution)/shard_map/convert_element_type | solution.py:32
  70.4 24.2 %all-gather.2.cloned.1.call-done = bf16[2048,8,128]{2,1,0:T(8,128)(2,1)} async-done(((bf16[32,8,128]{2,1,0:T(8,128)(2,1)}), bf16[2048,8,128]{2,1,0:T(8,128)(2,1)}) %all-gather.2.cloned.1.call-update) | async-done | bytes 4194320 | tf_op jit(solution)/shard_map/all_gather | solution.py:65
  94.6 6.9 %copy.16 = f32[256,8,8,128]{3,1,2,0:T(8,128)} copy(bf16[256,8,8,128]{3,2,1,0:T(8,128)(2,1)} %bitcast.30) | data formatting | bytes 12582912
  101.5 7.1 %gather_fusion = f32[512,1024]{1,0:T(8,128)} fusion(f32[2048,1024]{1,0:T(8,128)} %bitcast.26, s32[1024]{0:T(1024)S(1)} %pad_clamp_fusion), kind=kCustom, calls=%fused_computation | custom fusion | bytes 4196352 | tf_op jit(solution)/shard_map/jit(_take)/gather | solution.py:69
  108.6 2.3 fusion.45
  111.6 0.9 copy-done.3
  112.5 0.7 copy-done.1
  113.9 43.1 %fusion.46 = bf16[16,32,8,128]{3,2,1,0:T(8,128)(2,1)} fusion(f32[16,32,8,8]{3,2,1,0:T(8,128)} %get-tuple-element.31, f32[16,32,8,120]{3,2,1,0:T(8,128)} %get-tuple-element.33, f32[16,32,8,120]{3,2,1,0:T(8,128)} %get-tuple-element.32, f32[16,32,8,8]{3,2,1,0:T(8,128)} %get-tuple-element.30, f32[16,32,24,128]{3,2,1,0:T(8,128)} %maximum_convert_fusion, ...), kind=kLoop, calls=%fused_computation.85 | loop fusion | flops 39845888 | bytes 72351744 | tf_op jit(solution)/shard_map/convert_element_type | solution.py:77
  157.1 85.4 %reduce-scatter.2.cloned.1.call-done = f32[32,1024]{1,0:T(8,128)} async-done(((f32[2048,1024]{1,0:T(8,128)}), f32[32,1024]{1,0:T(8,128)}) %reduce-scatter.2.cloned.1.call-update) | async-done | bytes 131088 | tf_op jit(solution)/shard_map/reduce_scatter | solution.py:73
  242.5 1.6 copy.9
  (23 shorter events, 3.3 us)
Async XLA Ops:
  7.2 87.4 %all-gather.2.cloned.1.call-start = ((), (), s32[]{:S(2)}) async-start(), calls=%async_computation.1 | async-start | bytes 4259840 | tf_op jit(solution)/shard_map/all_gather | solution.py:65
  8.8 233.7 %reduce-scatter.2.cloned.1.call-start = ((), (), s32[]{:S(2)}) async-start(), calls=%async_computation.2 | async-start | bytes 8519680 | tf_op jit(solution)/shard_map/reduce_scatter | solution.py:73
  20.7 1.2 copy-start
  21.9 43.8 %collective-permute-start = (bf16[16,32,8,128]{3,2,1,0:T(8,128)(2,1)S(1)}, bf16[16,32,8,128]{3,2,1,0:T(8,128)(2,1)}, u32[]{:S(2)}, u32[]{:S(2)}) collective-permute-start(bf16[16,32,8,128]{3,2,1,0:T(8,128)(2,1)S(1)} %copy-done), channel_id=1, source_target_pairs={{0,1},{1,2},{2,3},{3,0},{4,5},{5,6},{6,7},{7,4},{8,9},{9,10},{10,1... | collective-permute-start | bytes 3145736 | tf_op jit(solution)/shard_map/ppermute | solution.py:21
  24.0 41.7 %collective-permute-start.1 = (bf16[16,32,8,128]{3,2,1,0:T(8,128)(2,1)S(1)}, bf16[16,32,8,128]{3,2,1,0:T(8,128)(2,1)}, u32[]{:S(2)}, u32[]{:S(2)}) collective-permute-start(bf16[16,32,8,128]{3,2,1,0:T(8,128)(2,1)S(1)} %copy-done), channel_id=1, source_target_pairs={{1,0},{2,1},{3,2},{0,3},{5,4},{6,5},{7,6},{4,7},{9,8},{10,9},{11,1... | collective-permute-start | bytes 3145736 | tf_op jit(solution)/shard_map/ppermute | solution.py:23
  108.6 3.0 %copy-start.4 = (f32[16,32,8,123]{3,2,1,0:T(8,128)S(1)}, f32[16,32,8,123]{3,2,1,0:T(8,128)}, u32[]{:S(2)}) copy-start(f32[16,32,8,123]{3,2,1,0:T(8,128)} %get-tuple-element.21) | copy-start | bytes 6045700
  110.9 1.7 copy-start.3
  111.1 2.1 copy-start.1
  111.1 2.8 %copy-start.2 = (f32[16,32,8,5]{3,2,1,0:T(8,128)S(1)}, f32[16,32,8,5]{3,2,1,0:T(8,128)}, u32[]{:S(2)}) copy-start(f32[16,32,8,5]{3,2,1,0:T(8,128)} %get-tuple-element.19) | copy-start | bytes 245764
Sparse Core Ops, SparseCore 0:
  11.3 83.1 all-gather.1
  98.8 143.6 reduce-scatter.1
where the time goes:
time: 255 us; the launch traced here: 251 us
  waiting for transfers between devices  110 us (43%)
  other arithmetic  62.7 us (25%)
  local copies, waits for them, and re-layouts  60.7 us (24%)
  between operations  14.1 us (6%)
  starting transfers between devices  3.65 us (1%)
    reduce_scatter x1, waiting for transfers between devices, on_device(): lax.psum_scatter(partial_value, 'grp', scatter_dimension=0, tiled=True)  85.4 us
    convert_element_type x1, other arithmetic, on_device(): applied = (-0.5 * laplace_term + potential_term.reshape(sf_count, box_row...  43.1 us
    slice x16, local copies, waits for them, and re-layouts, laplace_local(): along_z = jnp.roll(values, offset, 3) + jnp.roll(values, -offset, 3)  40.2 us
    all_gather x1, waiting for transfers between devices, on_device(): lax.all_gather(potential.astype(jnp.bfloat16), 'grp', axis=0, tiled=True)  24.2 us
    unnamed x13, local copies, waits for them, and re-layouts  12.5 us
    scatter-add x1, other arithmetic, on_device(): jnp.zeros((planes_all, cells), jnp.float32).at[plane].add(terms)  8.77 us
    gather x1, local copies, waits for them, and re-layouts, on_device(): jnp.take(whole, plane, axis=0) * rows_float  7.07 us
  transfers between devices with their start and end apart: 4, of which 2 were waited for; matrix products, arithmetic and copies ran while one was open for 47% of the time, Pallas kernels for 0%

commit v1 on v0

v1 whole, which is shorter than its diff:
```python
import functools
import math

import jax
import jax.numpy as jnp
import numpy as np
from jax import lax
from jax.experimental import pallas as pl
from jax.experimental.pallas import tpu as pltpu
from jax.sharding import PartitionSpec as P

MESH = pl.DeviceIdType.MESH
FUNCS, ROWS, LANES = 16, 256, 128
NXC, NZC = 4, 8
PAIRS = FUNCS // 2
TILE = 16
PLANES, TILES = ROWS // 8, ROWS // TILE
RA = 160
RB = ROWS - RA
HA, HB = RA // 2, RB // 2

kinetic_taps = [
    2.0 * (-1.0) ** (index + 2) / float((index + 1) * (index + 1)) for index in range(8)
]
center_tap = -math.pi * math.pi / 3.0


def split_bf16(matrix):
    high = matrix.astype(jnp.bfloat16)
    low = (matrix - high.astype(np.float64)).astype(jnp.bfloat16)
    return high, low


def stencil_matrices():
    along_y, along_x = np.zeros((32, 32)), np.zeros((8, 8))
    left, right, along_z = np.zeros((8, 8)), np.zeros((8, 8)), np.zeros((LANES, LANES))
    for offset in range(1, 9):
        weight = kinetic_taps[offset - 1]
        along_y += weight * (np.eye(32, k=offset) + np.eye(32, k=-offset))
        along_x += weight * (np.eye(8, k=offset) + np.eye(8, k=-offset))
        left += weight * np.eye(8, k=8 - offset)
        right += weight * np.eye(8, k=offset - 8)
        along_z += weight * (
            np.roll(np.eye(LANES), offset, 1) + np.roll(np.eye(LANES), -offset, 1)
        )
    own = (
        np.kron(along_y, np.eye(8))
        + np.kron(np.eye(32), along_x)
        + 3.0 * center_tap * np.eye(ROWS)
    )
    rows = np.concatenate(
        [own, np.kron(np.eye(32), left), np.kron(np.eye(32), right)], axis=1
    )
    rows_high, rows_low = split_bf16(-0.5 * rows)
    z_high, z_low = split_bf16(-0.5 * along_z)
    return np.stack([rows_high, rows_low]), np.concatenate([z_high, z_low], axis=0)


def kernel(
    corners, occupation, support, potential, row_weights_in, z_weights_in,
    applied, density,
    own, left, right, out, pot_in, dens, row_weights, z_weights,
    gathered, terms, table, part_out, part_in, sums,
    xa1, xa2, za1, za, zb1, zb, xb1, xb2,
    load_sem, out_sem, send_sem, recv_sem,
):
    f32, bf16 = jnp.float32, jnp.bfloat16
    group, slab = lax.axis_index("grp"), lax.axis_index("slab")
    x, z, core = group // 16, (group // 2) % 8, group % 2

    def chip(dx, dz):
        return ((((x + dx) % NXC) * NZC + (z + dz) % NZC) * 2 + core, slab)

    partner = (group + 1 - 2 * core, slab)
    x_next, x_prev = chip(1, 0), chip(NXC - 1, 0)
    z_next, z_prev = chip(0, 1), chip(0, NZC - 1)
    y_next, y_prev = (group, (slab + 1) % 4), (group, (slab + 3) % 4)
    along_x, along_z, along_y = (x_next, x_prev), (z_next, z_prev), (y_next, y_prev)

    loads = {}
    for index, (name, src, dst) in enumerate([
        ("potential", potential, pot_in),
        ("support", support, own),
        ("rows", row_weights_in, row_weights),
        ("z", z_weights_in, z_weights),
    ]):
        loads[name] = pltpu.make_async_copy(src, dst, load_sem.at[index])
        loads[name].start()

    sent = {}

    def send(name, src, dst, device):
        index = len(sent)
        copy = pltpu.make_async_remote_copy(
            src_ref=src, dst_ref=dst,
            send_sem=send_sem.at[index], recv_sem=recv_sem.at[index],
            device_id=device, device_id_type=MESH,
        )
        copy.start()
        sent[name] = copy

    def arrived(*name):
        sent[name].wait_recv()

    barrier = pltpu.get_barrier_semaphore()
    neighbours = (*along_x, *along_z, *along_y, partner)
    for device in neighbours:
        pl.semaphore_signal(barrier, inc=1, device_id=device, device_id_type=MESH)
    pl.semaphore_wait(barrier, len(neighbours))

    def slot(dx, dz, start, size):
        tiles = pl.ds(start // TILE, size // TILE)
        return gathered.at[(x + dx) % NXC, (z + dz) % NZC, core, tiles]

    def column(dz, start, size):
        tiles = pl.ds(start // TILE, size // TILE)
        return gathered.at[pl.ds(0, NXC), (z + dz) % NZC, core, tiles]

    def a_z(step):
        for way in range(2):
            dz = (NZC - (step - 1)) % NZC if way == 0 else step - 1
            where = slot(0, dz, 0, RA) if step < 4 else slot(0, dz, way * HA, HA)
            send(("az", step, way), where, where, along_z[way])

    def a_x1(dz):
        for way in range(2):
            where = slot(0, dz, 0, RA)
            send(("ax1", dz, way), where, where, along_x[way])

    def a_x2(dz):
        for way in range(2):
            arrived("ax1", dz, way)
            where = slot(3 if way == 0 else 1, dz, way * HA, HA)
            send(("ax2", dz, way), where, where, along_x[way])

    def a_partner(dz):
        for way in range(2):
            arrived("ax2", dz, way)
        where = column(dz, 0, RA)
        send(("ap", dz), where, where, partner)

    def b_x1():
        for way in range(2):
            where = slot(0, 0, RA, RB)
            send(("bx1", way), where, where, along_x[way])

    def b_x2():
        for way in range(2):
            arrived("bx1", way)
            where = slot(3 if way == 0 else 1, 0, RA + way * HB, HB)
            send(("bx2", way), where, where, along_x[way])

    def b_z(step):
        for way in range(2):
            dz = (NZC - (step - 1)) % NZC if way == 0 else step - 1
            where = column(dz, RA, RB) if step < 4 else column(dz, RA + way * HB, HB)
            send(("bz", step, way), where, where, along_z[way])

    def b_partner(dz):
        where = column(dz, RA, RB)
        send(("bp", dz), where, where, partner)

    def gather_step(step):
        if step == 0:
            a_z(1)
            a_x1(0)
            b_x1()
            return
        if step <= 4:
            for way in range(2):
                arrived("az", step, way)
            if step < 4:
                a_z(step + 1)
                a_x1(NZC - step)
                a_x1(step)
            else:
                a_x1(4)
        if step == 1:
            a_x2(0)
            b_x2()
        elif step <= 4:
            a_x2(NZC - step + 1)
            a_x2(step - 1)
        elif step == 5:
            a_x2(4)
        if step == 2:
            for way in range(2):
                arrived("bx2", way)
            b_z(1)
            b_partner(0)
            a_partner(0)
        elif step >= 3:
            for way in range(2):
                arrived("bz", step - 2, way)
            if step < 6:
                b_z(step - 1)
                b_partner(NZC - (step - 2))
                b_partner(step - 2)
                a_partner(NZC - (step - 2))
                a_partner(step - 2)
            else:
                b_partner(4)
                a_partner(4)

    def gather_end():
        for dz in range(NZC):
            arrived("ap", dz)
            arrived("bp", dz)
        gathered[4, 0, 0] = gathered[0, 0, 0]

    def build(target, dz, owner, added=None):
        shift = corners[0] % PLANES

        def one(dx, carry):
            block = ((x + dx) % NXC) * 16 + ((z + dz) % NZC) * 2 + owner
            after = table[block] - shift
            before = table[(block + 63) % 64] + PLANES - shift
            for at in range(0, PLANES, 2):
                planes = [
                    terms[plane + jnp.where(plane >= shift, after, before)]
                    for plane in (at, at + 1)
                ]
                value = jnp.concatenate(planes, axis=0)
                rows = pl.ds(at * 8, TILE)
                if added is not None:
                    value = value + added[dz, dx, rows, :].astype(f32)
                target[dz, dx, rows, :] = value.astype(bf16)
            return carry

        lax.fori_loop(0, NXC, one, 0)

    def build_partner(dz):
        build(part_out, dz, 1 - core)
        send(("part", dz), part_out.at[dz], part_in.at[dz], partner)

    def build_own(dz):
        arrived("part", dz)
        build(sums, dz, core, part_in)

    def add(where, start, size, *others):
        total = where[pl.ds(start, size), :].astype(f32)
        for other in others:
            total = total + other[...].astype(f32)
        where[pl.ds(start, size), :] = total.astype(bf16)

    def add4(dz, start, size, *others):
        for dx in range(NXC):
            add(sums.at[dz, dx], start, size, *[other.at[dx] for other in others])

    def ra_x1(dz):
        for way in range(2):
            send(("rax1", dz, way), sums.at[dz, 2, pl.ds(way * HA, HA)], xa1.at[dz, way], along_x[way])

    def ra_x2(dz):
        for way in range(2):
            dx = 1 if way == 0 else 3
            arrived("rax1", dz, way)
            add(sums.at[dz, dx], way * HA, HA, xa1.at[dz, way])
            send(("rax2", dz, way), sums.at[dz, dx, pl.ds(0, RA)], xa2.at[dz, way], along_x[way])

    def ra_x3(dz):
        for way in range(2):
            arrived("rax2", dz, way)
        add(sums.at[dz, 0], 0, RA, xa2.at[dz, 0], xa2.at[dz, 1])

    def ra_z(step):
        for way in range(2):
            if step == 1:
                send(("raz", 1, way), sums.at[4, 0, pl.ds(way * HA, HA)], za1.at[way], along_z[way])
                continue
            dz = 5 - step if way == 0 else 3 + step
            arrived("raz", step - 1, way)
            if step == 2:
                add(sums.at[dz, 0], way * HA, HA, za1.at[way])
            else:
                add(sums.at[dz, 0], 0, RA, za.at[step - 3, way])
            send(("raz", step, way), sums.at[dz, 0, pl.ds(0, RA)], za.at[step - 2, way], along_z[way])

    def rb_z(step):
        for way in range(2):
            if step == 1:
                send(("rbz", 1, way), sums.at[4, :, pl.ds(RA + way * HB, HB)], zb1.at[way], along_z[way])
                continue
            dz = 5 - step if way == 0 else 3 + step
            arrived("rbz", step - 1, way)
            if step == 2:
                add4(dz, RA + way * HB, HB, zb1.at[way])
            else:
                add4(dz, RA, RB, zb.at[step - 3, way])
            send(("rbz", step, way), sums.at[dz, :, pl.ds(RA, RB)], zb.at[step - 2, way], along_z[way])

    def rb_x1():
        for way in range(2):
            arrived("rbz", 4, way)
        add4(0, RA, RB, zb.at[2, 0], zb.at[2, 1])
        for way in range(2):
            send(("rbx1", way), sums.at[0, 2, pl.ds(RA + way * HB, HB)], xb1.at[way], along_x[way])

    def rb_x2():
        for way in range(2):
            dx = 1 if way == 0 else 3
            arrived("rbx1", way)
            add(sums.at[0, dx], RA + way * HB, HB, xb1.at[way])
            send(("rbx2", way), sums.at[0, dx, pl.ds(RA, RB)], xb2.at[way], along_x[way])

    levels = [(4,), (3, 5), (2, 6), (1, 7), (0,)]

    def scatter_step(step):
        if step <= 3:
            rb_z(step + 1)
        elif step == 4:
            rb_x1()
        elif step == 5:
            rb_x2()
        if step >= 2:
            for dz in levels[step - 2]:
                ra_x3(dz)
            if step < 6:
                ra_z(step - 1)
        if 1 <= step <= 5:
            for dz in levels[step - 1]:
                ra_x2(dz)
        if step <= 4:
            for dz in levels[step]:
                ra_x1(dz)

    def scatter_end():
        for way in range(2):
            arrived("raz", 4, way)
        dens[pl.ds(0, RA), :] = (
            sums[0, 0, pl.ds(0, RA), :].astype(f32)
            + za[2, 0].astype(f32) + za[2, 1].astype(f32)
        )
        for way in range(2):
            arrived("rbx2", way)
        dens[pl.ds(RA, RB), :] = (
            sums[0, 0, pl.ds(RA, RB), :].astype(f32)
            + xb2[0].astype(f32) + xb2[1].astype(f32)
        )
        copy = pltpu.make_async_copy(dens, density, out_sem.at[PAIRS])
        copy.start()
        loads["density"] = copy

    def apply(pair):
        arrived("halo", pair, 0)
        arrived("halo", pair, 1)
        first = 2 * pair
        both = [
            jnp.concatenate([ref[first], ref[first + 1]], axis=1) for ref in (own, left, right)
        ]
        cells = jnp.concatenate(both, axis=0)
        total = jnp.dot(row_weights[0], cells, preferred_element_type=f32)
        total = total + jnp.dot(row_weights[1], cells, preferred_element_type=f32)
        flat = gathered.reshape(5 * NZC * 2 * TILES, TILE, LANES)
        for index in range(2):
            values = own[first + index]
            twice = jnp.concatenate([values, values], axis=1)
            result = total[:, index * LANES:(index + 1) * LANES] + jnp.dot(
                twice, z_weights[...], preferred_element_type=f32
            )
            corner = corners[first + index]
            window = flat[pl.ds(corner // 2, TILES + 1)].astype(f32).reshape(ROWS + TILE, LANES)
            local = jnp.where(corner % 2 == 1, window[8:8 + ROWS], window[:ROWS])
            term = (local * values.astype(f32)).astype(bf16).astype(f32)
            out[first + index] = (result + term).astype(bf16)
        copy = pltpu.make_async_copy(
            out.at[pl.ds(first, 2)], applied.at[pl.ds(first, 2)], out_sem.at[pair]
        )
        copy.start()
        loads["out", pair] = copy

    loads["potential"].wait()
    gathered[x, z, core] = pot_in[...].astype(bf16).reshape(TILES, TILE, LANES)
    gather_step(0)
    for pair in range(PAIRS):
        where = pl.ds(2 * pair, 2)
        send(("halo", pair, 0), support.at[where], left.at[where], y_next)
        send(("halo", pair, 1), support.at[where], right.at[where], y_prev)

    bases = [corners[k] // 32 for k in range(FUNCS)]

    def find(block, carry):
        found = FUNCS
        for k in reversed(range(FUNCS)):
            found = jnp.where(bases[k] == block, k, found)
        table[block] = found * PLANES
        return carry

    lax.fori_loop(0, 64, find, 0)
    terms[pl.ds(FUNCS * PLANES, PLANES)] = jnp.zeros((PLANES, 8, LANES), f32)
    loads["support"].wait()
    for k in range(FUNCS):
        value = own[k].astype(f32)
        twin = k
        for other in reversed(range(k + 1, FUNCS)):
            twin = jnp.where(bases[other] == bases[k], other, twin)
        total = occupation[k] * value * value
        if k + 1 < FUNCS:
            second = own[twin].astype(f32)
            weight = jnp.where(twin == k, 0.0, occupation[twin])
            total = total + weight * second * second
        terms[pl.ds(k * PLANES, PLANES)] = total.reshape(PLANES, 8, LANES)
    gather_step(1)
    for dz in levels[0] + levels[1]:
        build_partner(dz)
    gather_step(2)
    build_own(4)
    scatter_step(0)
    for level in range(1, 5):
        if level < 4:
            for dz in levels[level + 1]:
                build_partner(dz)
        for dz in levels[level]:
            build_own(dz)
        scatter_step(level)
        if level < 4:
            gather_step(level + 2)
    gather_step(6)
    scatter_step(5)
    gather_end()
    loads["rows"].wait()
    loads["z"].wait()
    for pair in range(3):
        apply(pair)
    scatter_step(6)
    scatter_end()
    for pair in range(3, PAIRS):
        apply(pair)
    for copy in sent.values():
        copy.wait_send()
    for pair in range(PAIRS):
        loads["out", pair].wait()
    loads["density"].wait()


def on_device(support, corners, occupation, potential):
    rows, z_mix = stencil_matrices()
    bf16, f32 = jnp.bfloat16, jnp.float32
    vmem = lambda shape, kind=bf16: pltpu.VMEM(shape, kind)
    smem = pl.BlockSpec(memory_space=pltpu.SMEM)
    anywhere = pl.BlockSpec(memory_space=pl.ANY)
    copies = 160
    applied, density = pl.pallas_call(
        kernel,
        out_shape=(
            jax.ShapeDtypeStruct((FUNCS, ROWS, LANES), bf16),
            jax.ShapeDtypeStruct((ROWS, LANES), f32),
        ),
        in_specs=[smem, smem, anywhere, anywhere, anywhere, anywhere],
        out_specs=(anywhere, anywhere),
        scratch_shapes=[
            vmem((FUNCS, ROWS, LANES)),
            vmem((FUNCS, ROWS, LANES)),
            vmem((FUNCS, ROWS, LANES)),
            vmem((FUNCS, ROWS, LANES)),
            vmem((ROWS, LANES), f32),
            vmem((ROWS, LANES), f32),
            vmem(rows.shape),
            vmem(z_mix.shape),
            vmem((NXC + 1, NZC, 2, TILES, TILE, LANES)),
            vmem(((FUNCS + 1) * PLANES, 8, LANES), f32),
            pltpu.SMEM((64,), jnp.int32),
            vmem((NZC, NXC, ROWS, LANES)),
            vmem((NZC, NXC, ROWS, LANES)),
            vmem((NZC, NXC, ROWS, LANES)),
            vmem((NZC, 2, HA, LANES)),
            vmem((NZC, 2, RA, LANES)),
            vmem((2, HA, LANES)),
            vmem((3, 2, RA, LANES)),
            vmem((2, NXC, HB, LANES)),
            vmem((3, 2, NXC, RB, LANES)),
            vmem((2, HB, LANES)),
            vmem((2, RB, LANES)),
            pltpu.SemaphoreType.DMA((4,)),
            pltpu.SemaphoreType.DMA((PAIRS + 1,)),
            pltpu.SemaphoreType.DMA((copies,)),
            pltpu.SemaphoreType.DMA((copies,)),
        ],
        compiler_params=pltpu.CompilerParams(
            collective_id=0, has_side_effects=True, vmem_limit_bytes=48 * 1024 * 1024
        ),
    )(
        corners,
        occupation.astype(f32),
        support.reshape(FUNCS, ROWS, LANES),
        potential.reshape(ROWS, LANES),
        jnp.asarray(rows),
        jnp.asarray(z_mix),
    )
    return applied.reshape(support.shape), density.reshape(potential.shape)


def solution(mesh):
    in_specs = (P("grp", None, "slab", None), P("grp"), P("grp"), P("grp", "slab", None))
    out_specs = (P("grp", None, "slab", None), P("grp", "slab", None))
    return jax.shard_map(
        on_device, mesh=mesh, in_specs=in_specs, out_specs=out_specs, check_vma=False
    )
```

time: 255 us -> 60 us (0.24)
  the two profiles are of different devices: /device:TPU:1 before, /device:TPU:8 now
where the time goes in v1:
time: 60 us; the launch traced here: 59.8 us
  Pallas kernels  52.1 us (87%)
  local copies, waits for them, and re-layouts  7.03 us (12%)
  between operations  0.65 us (1%)
    pallas_call x1, Pallas kernels, on_device(): pl.pallas_call(kernel, out_shape=(jax.ShapeDtypeStruct((FUNCS, ROWS, LANE...  52.1 us
    unnamed x14, local copies, waits for them, and re-layouts  7.03 us

profile of v1, /device:TPU:8, one launch (start us, length us, event | category | flops | bytes accessed | tf_op | source)
XLA Modules:
  0.0 59.8 jit_solution(7844663018518004204)
XLA Ops:
  0.6 0.0 copy-start.5
  0.6 0.6 %copy-done.5 = bf16[16]{0:T(256)(128)(2,1)S(1)} copy-done((bf16[16]{0:T(256)(128)(2,1)S(1)}, bf16[16]{0:T(256)(128)(2,1)}, u32[]{:S(2)}) %copy-start.5) | copy-done | bytes 56
  1.3 0.0 copy-start.4
  1.3 0.7 %copy-done.4 = s32[16]{0:T(128)S(1)} copy-done((s32[16]{0:T(128)S(1)}, s32[16]{0:T(128)}, u32[]{:S(2)}) %copy-start.4) | copy-done | bytes 88
  1.9 0.0 copy-start
  1.9 1.2 %copy-done = bf16[16,32,8,128]{3,2,1,0:T(8,128)(2,1)S(1)} copy-done((bf16[16,32,8,128]{3,2,1,0:T(8,128)(2,1)S(1)}, bf16[16,32,8,128]{3,2,1,0:T(8,128)(2,1)}, u32[]{:S(2)}) %copy-start) | copy-done | bytes 1048600
  3.2 0.0 copy-start.1
  3.2 1.1 %copy-done.1 = bf16[2,256,768]{2,1,0:T(8,128)(2,1)S(1)} copy-done((bf16[2,256,768]{2,1,0:T(8,128)(2,1)S(1)}, bf16[2,256,768]{2,1,0:T(8,128)(2,1)}, u32[]{:S(2)}) %copy-start.1) | copy-done | bytes 786456
  4.3 0.0 copy-start.2
  4.3 0.9 %copy-done.2 = f32[32,8,128]{2,1,0:T(8,128)S(1)} copy-done((f32[32,8,128]{2,1,0:T(8,128)S(1)}, f32[32,8,128]{2,1,0:T(8,128)}, u32[]{:S(2)}) %copy-start.2) | copy-done | bytes 131096
  5.2 0.0 copy-start.3
  5.2 0.8 %copy-done.3 = bf16[256,128]{1,0:T(8,128)(2,1)S(1)} copy-done((bf16[256,128]{1,0:T(8,128)(2,1)S(1)}, bf16[256,128]{1,0:T(8,128)(2,1)}, u32[]{:S(2)}) %copy-start.3) | copy-done | bytes 65560
  6.0 52.1 %shard_map.77 = (bf16[16,256,128]{2,1,0:T(8,128)(2,1)S(1)}, f32[256,128]{1,0:T(8,128)S(1)}) custom-call(s32[16]{0:T(128)S(1)} %copy-done.4, f32[16]{0:T(128)S(1)} %convert_element_type.3.occupation, bf16[16,256,128]{2,1,0:T(8,128)(2,1)S(1)} %bitcast.4, f32[256,128]{1,0:T(8,128)S(1)} %bitcast.6, bf16[2,256,768]{2,1,0:T(8,128)(2,1)S(1)} %copy-done.1, ...), custom_call_target="tpu_custom_call" | custom-call | tf_op jit(solution)/shard_map/pallas_call | solution.py:443
  58.2 1.0 %copy.10 = bf16[16,32,8,128]{3,2,1,0:T(8,128)(2,1)} copy(bf16[16,32,8,128]{3,2,1,0:T(8,128)(2,1)S(1)} %bitcast.5) | data formatting | bytes 2097152
  59.1 0.7 %copy.11 = f32[32,8,128]{2,1,0:T(8,128)} copy(f32[32,8,128]{2,1,0:T(8,128)S(1)} %bitcast.7) | data formatting | bytes 262144
  (1 shorter events, 0.0 us)
Async XLA Ops:
  0.6 0.7 %copy-start.5 = (bf16[16]{0:T(256)(128)(2,1)S(1)}, bf16[16]{0:T(256)(128)(2,1)}, u32[]{:S(2)}) copy-start(bf16[16]{0:T(256)(128)(2,1)} %param.8) | copy-start | bytes 100
  1.3 0.7 %copy-start.4 = (s32[16]{0:T(128)S(1)}, s32[16]{0:T(128)}, u32[]{:S(2)}) copy-start(s32[16]{0:T(128)} %corners.1) | copy-start | bytes 196
  1.9 1.2 %copy-start = (bf16[16,32,8,128]{3,2,1,0:T(8,128)(2,1)S(1)}, bf16[16,32,8,128]{3,2,1,0:T(8,128)(2,1)}, u32[]{:S(2)}) copy-start(bf16[16,32,8,128]{3,2,1,0:T(8,128)(2,1)} %param.6) | copy-start | bytes 3145732
  3.2 1.1 %copy-start.1 = (bf16[2,256,768]{2,1,0:T(8,128)(2,1)S(1)}, bf16[2,256,768]{2,1,0:T(8,128)(2,1)}, u32[]{:S(2)}) copy-start(bf16[2,256,768]{2,1,0:T(8,128)(2,1)} %constant.4.clone.row_weights_in) | copy-start | bytes 2359300
  4.3 0.9 %copy-start.2 = (f32[32,8,128]{2,1,0:T(8,128)S(1)}, f32[32,8,128]{2,1,0:T(8,128)}, u32[]{:S(2)}) copy-start(f32[32,8,128]{2,1,0:T(8,128)} %param.9) | copy-start | bytes 393220
  5.2 0.8 %copy-start.3 = (bf16[256,128]{1,0:T(8,128)(2,1)S(1)}, bf16[256,128]{1,0:T(8,128)(2,1)}, u32[]{:S(2)}) copy-start(bf16[256,128]{1,0:T(8,128)(2,1)} %constant.5.clone.z_weights_in) | copy-start | bytes 196612

commit v2 on v1

v2 whole, which is shorter than its diff:
```python
import functools
import math

import jax
import jax.numpy as jnp
import numpy as np
from jax import lax
from jax.experimental import pallas as pl
from jax.experimental.pallas import tpu as pltpu
from jax.sharding import PartitionSpec as P

MESH = pl.DeviceIdType.MESH
FUNCS, ROWS, LANES = 16, 256, 128
NXC, NZC = 4, 8
PAIRS = FUNCS // 2
TILE = 16
PLANES, TILES = ROWS // 8, ROWS // TILE
RA = 160
RB = ROWS - RA
HA, HB = RA // 2, RB // 2

kinetic_taps = [
    2.0 * (-1.0) ** (index + 2) / float((index + 1) * (index + 1)) for index in range(8)
]
center_tap = -math.pi * math.pi / 3.0


ORDER = (
    ("bx1",), ("az", 1, 0), ("az", 1, 1), ("bpart", 4), ("ax1", 0), ("halo",), ("bpart", 5), ("bx2", 0),
    ("bx2", 1), ("bown", 4), ("rax1", 4), ("rbz", 2, 1), ("ax1", 7), ("az", 2, 1), ("bpart", 3), ("az", 2, 0),
    ("rbz", 0, 1), ("rbz", 3, 1), ("bpart", 2), ("ax1", 1), ("bown", 5), ("rax1", 5), ("rbz", 1, 1),
    ("bpart", 6), ("bown", 3), ("rax1", 3), ("bz", 1, 1), ("bz", 1, 0), ("ax2", 0, 0), ("ax2", 0, 1),
    ("rbz", 2, 2, 0), ("rax2", 4, 1), ("rax2", 4, 0), ("bown", 2), ("bpart", 7), ("rax1", 2),
    ("rbz", 2, 2, 1), ("bown", 6), ("bpart", 0), ("az", 3, 1), ("az", 3, 0), ("rax1", 6), ("ax1", 6),
    ("bpart", 1), ("ax2", 1, 0), ("rbz", 1, 2, 0), ("rax2", 3, 1), ("rbz", 3, 2, 0), ("rbz", 3, 2, 1),
    ("rax2", 3, 0), ("rbz", 1, 2, 1), ("rbz", 0, 2, 0), ("ax2", 1, 1), ("bown", 0), ("rax2", 5, 0),
    ("ax1", 2), ("rax2", 5, 1), ("ax2", 7, 1), ("rbz", 0, 2, 1), ("bown", 7), ("rax1", 7), ("rax3", 4),
    ("raz", 1), ("rbz", 2, 3, 0), ("rbz", 2, 3, 1), ("rax2", 2, 1), ("rax2", 6, 0), ("bz", 2, 1),
    ("bz", 2, 0), ("bown", 1), ("rax1", 1), ("lap", 2), ("rbz", 1, 3, 1), ("rax3", 3), ("rax2", 2, 0),
    ("az", 4, 0), ("ax2", 6, 0), ("az", 4, 1), ("raz", 2, 0), ("rax2", 6, 1), ("rbz", 1, 3, 0),
    ("rbz", 2, 4, 1), ("lap", 0), ("ax1", 5), ("rbz", 2, 4, 0), ("rbz", 3, 3, 0), ("ax2", 6, 1),
    ("rbz", 3, 3, 1), ("lap", 3), ("rax3", 5), ("ax2", 2, 1), ("raz", 2, 1), ("ax1", 3), ("bz", 3, 1),
    ("ax2", 7, 0), ("rbz", 0, 3, 1), ("bp", 0), ("bz", 3, 0), ("rax2", 7, 0), ("bp", 2, 0), ("ax1", 4),
    ("rbz", 1, 4, 1), ("rax1", 0), ("rbz", 0, 3, 0), ("rax2", 1, 0), ("ap", 1), ("ax2", 2, 0), ("rax2", 7, 1),
    ("rax3", 2), ("raz", 3, 0), ("rax3", 6), ("raz", 3, 1), ("rbz", 1, 4, 0), ("rbz", 3, 4, 0),
    ("rax2", 1, 1), ("rbx1",), ("bp", 1, 0), ("ax2", 5, 0), ("ax2", 5, 1), ("rbz", 3, 4, 1), ("lap", 1),
    ("ax2", 3, 0), ("bp", 3, 0), ("ax2", 3, 1), ("bz", 4, 0), ("bz", 4, 1), ("ax2", 4, 0), ("ap", 0),
    ("ax2", 4, 1), ("bp", 2, 1), ("ap", 6), ("rbz", 0, 4, 0), ("rbz", 0, 4, 1), ("rax2", 0, 1),
    ("rax2", 0, 0), ("rax3", 7), ("raz", 4, 1), ("ap", 7), ("ap", 2), ("rax3", 1), ("raz", 4, 0), ("rbx2", 1),
    ("bp", 1, 1), ("rbx2", 0), ("ap", 5), ("lap", 4), ("bp", 3, 1), ("ap", 3), ("ap", 4), ("bp", 4),
    ("lap", 5), ("rax3", 0), ("lap", 6), ("lap", 7), ("agend",), ("fin", 6), ("fin", 0), ("fin", 3),
    ("fin", 2), ("fin", 1), ("fin", 7), ("fin", 4), ("fin", 5), ("rsend",),
)


def split_bf16(matrix):
    high = matrix.astype(jnp.bfloat16)
    low = (matrix - high.astype(np.float64)).astype(jnp.bfloat16)
    return high, low


def stencil_matrices():
    along_y, along_x = np.zeros((32, 32)), np.zeros((8, 8))
    left, right, along_z = np.zeros((8, 8)), np.zeros((8, 8)), np.zeros((LANES, LANES))
    for offset in range(1, 9):
        weight = kinetic_taps[offset - 1]
        along_y += weight * (np.eye(32, k=offset) + np.eye(32, k=-offset))
        along_x += weight * (np.eye(8, k=offset) + np.eye(8, k=-offset))
        left += weight * np.eye(8, k=8 - offset)
        right += weight * np.eye(8, k=offset - 8)
        along_z += weight * (
            np.roll(np.eye(LANES), offset, 1) + np.roll(np.eye(LANES), -offset, 1)
        )
    own = (
        np.kron(along_y, np.eye(8))
        + np.kron(np.eye(32), along_x)
        + 3.0 * center_tap * np.eye(ROWS)
    )
    rows = np.concatenate(
        [own, np.kron(np.eye(32), left), np.kron(np.eye(32), right)], axis=1
    )
    rows_high, rows_low = split_bf16(-0.5 * rows)
    z_high, z_low = split_bf16(-0.5 * along_z)
    halves = [part[:, at:at + LANES] for part in (rows_high, rows_low) for at in range(0, 3 * ROWS, LANES)]
    mixes = np.stack([*halves, np.concatenate([z_high, z_low], axis=0)])
    return mixes.reshape(len(mixes), PLANES, 8, LANES)


def kernel(
    corners, occupation, support, potential, mixes_in,
    applied, density,
    own, left, right, out, pot_in, dens, mixes,
    kinetic, gathered, terms, table, part_out, part_in, sums,
    xa1, xa2, za1, za, zb1, zb, xb1, xb2,
    load_sem, out_sem, send_sem, recv_sem,
):
    f32, bf16 = jnp.float32, jnp.bfloat16
    group, slab = lax.axis_index("grp"), lax.axis_index("slab")
    x, z, core = group // 16, (group // 2) % 8, group % 2

    def chip(dx, dz):
        return ((((x + dx) % NXC) * NZC + (z + dz) % NZC) * 2 + core, slab)

    partner = (group + 1 - 2 * core, slab)
    x_next, x_prev = chip(1, 0), chip(NXC - 1, 0)
    z_next, z_prev = chip(0, 1), chip(0, NZC - 1)
    y_next, y_prev = (group, (slab + 1) % 4), (group, (slab + 3) % 4)
    along_x, along_z, along_y = (x_next, x_prev), (z_next, z_prev), (y_next, y_prev)

    loads = {}
    for index, (name, src, dst) in enumerate([
        ("potential", potential, pot_in),
        ("support", support, own),
        ("mixes", mixes_in.reshape(mixes.shape), mixes),
    ]):
        loads[name] = pltpu.make_async_copy(src, dst, load_sem.at[index])
        loads[name].start()

    sent, pending = {}, set()

    def send(name, src, dst, device):
        index = len(sent)
        copy = pltpu.make_async_remote_copy(
            src_ref=src, dst_ref=dst,
            send_sem=send_sem.at[index], recv_sem=recv_sem.at[index],
            device_id=device, device_id_type=MESH,
        )
        copy.start()
        sent[name] = copy
        pending.add(name)

    barrier = pltpu.get_barrier_semaphore()
    neighbours = (*along_x, *along_z, *along_y, partner)
    for device in neighbours:
        pl.semaphore_signal(barrier, inc=1, device_id=device, device_id_type=MESH)

    def arrived(*name):
        if name in pending:
            pending.remove(name)
            sent[name].wait_recv()

    def slot(dx, dz, start, size):
        tiles = pl.ds(start // TILE, size // TILE)
        return gathered.at[(x + dx) % NXC, (z + dz) % NZC, core, tiles]

    def column(dz, start, size):
        tiles = pl.ds(start // TILE, size // TILE)
        return gathered.at[pl.ds(0, NXC), (z + dz) % NZC, core, tiles]

    def from_way(way, distance):
        return (NZC - distance) % NZC if way == 0 else distance

    def az(step, way):
        if step > 1:
            arrived("az", step - 1, way)
        dz = from_way(way, step - 1)
        where = slot(0, dz, 0, RA) if step < 4 else slot(0, dz, way * HA, HA)
        send(("az", step, way), where, where, along_z[way])

    def ax1(dz):
        if dz == 4:
            arrived("az", 4, 0)
            arrived("az", 4, 1)
        elif dz:
            arrived("az", min(dz, NZC - dz), 0 if dz > 4 else 1)
        for way in range(2):
            where = slot(0, dz, 0, RA)
            send(("ax1", dz, way), where, where, along_x[way])

    def ax2(dz, way):
        arrived("ax1", dz, way)
        where = slot(3 if way == 0 else 1, dz, way * HA, HA)
        send(("ax2", dz, way), where, where, along_x[way])

    def ap(dz):
        for way in range(2):
            arrived("ax2", dz, way)
        where = column(dz, 0, RA)
        send(("ap", dz), where, where, partner)

    def bx1():
        for way in range(2):
            where = slot(0, 0, RA, RB)
            send(("bx1", way), where, where, along_x[way])

    def bx2(way):
        arrived("bx1", way)
        where = slot(3 if way == 0 else 1, 0, RA + way * HB, HB)
        send(("bx2", way), where, where, along_x[way])

    def bz(step, way):
        if step == 1:
            arrived("bx2", 0)
            arrived("bx2", 1)
        else:
            arrived("bz", step - 1, way)
        dz = from_way(way, step - 1)
        where = column(dz, RA, RB) if step < 4 else column(dz, RA + way * HB, HB)
        send(("bz", step, way), where, where, along_z[way])

    def bp(distance, way=0):
        if distance == 0:
            arrived("bx2", 0)
            arrived("bx2", 1)
        elif distance == 4:
            arrived("bz", 4, 0)
            arrived("bz", 4, 1)
        else:
            arrived("bz", distance, way)
        dz = from_way(way, distance)
        where = column(dz, RA, RB)
        send(("bp", dz), where, where, partner)

    def agend():
        for dz in range(NZC):
            arrived("ap", dz)
            arrived("bp", dz)
        gathered[4, 0, 0] = gathered[0, 0, 0]

    def build(target, dz, owner, added=None):
        shift = corners[0] % PLANES

        def one(dx, carry):
            block = ((x + dx) % NXC) * 16 + ((z + dz) % NZC) * 2 + owner
            after = table[block] - shift
            before = table[(block + 63) % 64] + PLANES - shift
            for at in range(0, PLANES, 2):
                planes = [
                    terms[plane + jnp.where(plane >= shift, after, before)]
                    for plane in (at, at + 1)
                ]
                value = jnp.concatenate(planes, axis=0)
                rows = pl.ds(at * 8, TILE)
                if added is not None:
                    value = value + added[dz, dx, rows, :].astype(f32)
                target[dz, dx, rows, :] = value.astype(bf16)
            return carry

        lax.fori_loop(0, NXC, one, 0)

    def bpart(dz):
        build(part_out, dz, 1 - core)
        send(("part", dz), part_out.at[dz], part_in.at[dz], partner)

    def bown(dz):
        arrived("part", dz)
        build(sums, dz, core, part_in)

    def add(where, start, size, *others):
        total = where[pl.ds(start, size), :].astype(f32)
        for other in others:
            total = total + other[...].astype(f32)
        where[pl.ds(start, size), :] = total.astype(bf16)

    def rax1(dz):
        for way in range(2):
            part = sums.at[dz, 2, pl.ds(way * HA, HA)]
            send(("rax1", dz, way), part, xa1.at[dz, way], along_x[way])

    def rax2(dz, way):
        dx = 1 if way == 0 else 3
        arrived("rax1", dz, way)
        add(sums.at[dz, dx], way * HA, HA, xa1.at[dz, way])
        part = sums.at[dz, dx, pl.ds(0, RA)]
        send(("rax2", dz, way), part, xa2.at[dz, way], along_x[way])

    def rax3(dz):
        for way in range(2):
            arrived("rax2", dz, way)
        add(sums.at[dz, 0], 0, RA, xa2.at[dz, 0], xa2.at[dz, 1])

    def raz(step, way=None):
        if step == 1:
            for way in range(2):
                part = sums.at[4, 0, pl.ds(way * HA, HA)]
                send(("raz", 1, way), part, za1.at[way], along_z[way])
            return
        dz = 5 - step if way == 0 else 3 + step
        arrived("raz", step - 1, way)
        if step == 2:
            add(sums.at[dz, 0], way * HA, HA, za1.at[way])
        else:
            add(sums.at[dz, 0], 0, RA, za.at[step - 3, way])
        part = sums.at[dz, 0, pl.ds(0, RA)]
        send(("raz", step, way), part, za.at[step - 2, way], along_z[way])

    def rbz(dx, step, way=None):
        if step == 1:
            for way in range(2):
                part = sums.at[4, dx, pl.ds(RA + way * HB, HB)]
                send(("rbz", dx, 1, way), part, zb1.at[way, dx], along_z[way])
            return
        dz = 5 - step if way == 0 else 3 + step
        arrived("rbz", dx, step - 1, way)
        if step == 2:
            add(sums.at[dz, dx], RA + way * HB, HB, zb1.at[way, dx])
        else:
            add(sums.at[dz, dx], RA, RB, zb.at[step - 3, way, dx])
        part = sums.at[dz, dx, pl.ds(RA, RB)]
        send(("rbz", dx, step, way), part, zb.at[step - 2, way, dx], along_z[way])

    def rbz_end(dx):
        for way in range(2):
            arrived("rbz", dx, 4, way)
        add(sums.at[0, dx], RA, RB, zb.at[2, 0, dx], zb.at[2, 1, dx])

    def rbx1():
        rbz_end(2)
        for way in range(2):
            part = sums.at[0, 2, pl.ds(RA + way * HB, HB)]
            send(("rbx1", way), part, xb1.at[way], along_x[way])

    def rbx2(way):
        dx = 1 if way == 0 else 3
        rbz_end(dx)
        arrived("rbx1", way)
        add(sums.at[0, dx], RA + way * HB, HB, xb1.at[way])
        send(("rbx2", way), sums.at[0, dx, pl.ds(RA, RB)], xb2.at[way], along_x[way])

    def rsend():
        for way in range(2):
            arrived("raz", 4, way)
            for dx in range(NXC):
                arrived("rbz", dx, 4, way)
            arrived("rbx2", way)
        dens[pl.ds(0, RA), :] = (
            sums[0, 0, pl.ds(0, RA), :].astype(f32)
            + za[2, 0].astype(f32) + za[2, 1].astype(f32)
        )
        dens[pl.ds(RA, RB), :] = (
            sums[0, 0, pl.ds(RA, RB), :].astype(f32)
            + zb[2, 0, 0].astype(f32) + zb[2, 1, 0].astype(f32)
            + xb2[0].astype(f32) + xb2[1].astype(f32)
        )
        loads["density"] = pltpu.make_async_copy(dens, density, out_sem.at[PAIRS])
        loads["density"].start()

    def halo():
        for pair in range(PAIRS):
            where = pl.ds(2 * pair, 2)
            send(("halo", pair, 0), support.at[where], left.at[where], y_next)
            send(("halo", pair, 1), support.at[where], right.at[where], y_prev)

    def lap(pair):
        if pair == first_lap:
            loads["mixes"].wait()
        arrived("halo", pair, 0)
        arrived("halo", pair, 1)
        first = 2 * pair
        cells = jnp.concatenate([
            jnp.concatenate([ref[first], ref[first + 1]], axis=1) for ref in (own, left, right)
        ], axis=0)
        high, low = (
            jnp.concatenate([mixes[at + piece] for piece in range(6)], axis=1) for at in (0, 6)
        )
        total = jnp.dot(high, cells, preferred_element_type=f32)
        total = total + jnp.dot(low, cells, preferred_element_type=f32)
        for index in range(2):
            values = own[first + index]
            twice = jnp.concatenate([values, values], axis=1)
            kinetic[first + index] = total[:, index * LANES:(index + 1) * LANES] + jnp.dot(
                twice, mixes[12], preferred_element_type=f32
            )

    def fin(pair):
        first = 2 * pair
        flat = gathered.reshape(5 * NZC * 2 * TILES, TILE, LANES)
        for func in (first, first + 1):
            corner = corners[func]
            window = flat[pl.ds(corner // 2, TILES + 1)].astype(f32).reshape(ROWS + TILE, LANES)
            local = jnp.where(corner % 2 == 1, window[8:8 + ROWS], window[:ROWS])
            term = (local * own[func].astype(f32)).astype(bf16).astype(f32)
            out[func] = (kinetic[func] + term).astype(bf16)
        loads["out", pair] = pltpu.make_async_copy(
            out.at[pl.ds(first, 2)], applied.at[pl.ds(first, 2)], out_sem.at[pair]
        )
        loads["out", pair].start()

    bases = [corners[k] // 32 for k in range(FUNCS)]

    def find(block, carry):
        found = FUNCS
        for k in reversed(range(FUNCS)):
            found = jnp.where(bases[k] == block, k, found)
        table[block] = found * PLANES
        return carry

    lax.fori_loop(0, 64, find, 0)
    terms[pl.ds(FUNCS * PLANES, PLANES)] = jnp.zeros((PLANES, 8, LANES), f32)
    loads["potential"].wait()
    gathered[x, z, core] = pot_in[...].astype(bf16).reshape(TILES, TILE, LANES)
    loads["support"].wait()
    for k in range(FUNCS):
        value = own[k].astype(f32)
        twin = k
        for other in reversed(range(k + 1, FUNCS)):
            twin = jnp.where(bases[other] == bases[k], other, twin)
        total = occupation[k] * value * value
        if k + 1 < FUNCS:
            second = own[twin].astype(f32)
            weight = jnp.where(twin == k, 0.0, occupation[twin])
            total = total + weight * second * second
        terms[pl.ds(k * PLANES, PLANES)] = total.reshape(PLANES, 8, LANES)
    pl.semaphore_wait(barrier, len(neighbours))

    steps = {step.__name__: step for step in (
        az, ax1, ax2, ap, bx1, bx2, bz, bp, agend, bpart, bown, rax1, rax2, rax3,
        raz, rbz, rbx1, rbx2, rsend, halo, lap, fin,
    )}
    first_lap = next(args[0] for name, *args in ORDER if name == "lap")
    for name, *args in ORDER:
        steps[name](*args)
    for copy in sent.values():
        copy.wait_send()
    for pair in range(PAIRS):
        loads["out", pair].wait()
    loads["density"].wait()


def on_device(support, corners, occupation, potential):
    mixes = stencil_matrices()
    bf16, f32 = jnp.bfloat16, jnp.float32
    vmem = lambda shape, kind=bf16: pltpu.VMEM(shape, kind)
    smem = pl.BlockSpec(memory_space=pltpu.SMEM)
    anywhere = pl.BlockSpec(memory_space=pl.ANY)
    copies = 192
    applied, density = pl.pallas_call(
        kernel,
        out_shape=(
            jax.ShapeDtypeStruct((FUNCS, ROWS, LANES), bf16),
            jax.ShapeDtypeStruct((ROWS, LANES), f32),
        ),
        in_specs=[smem, smem, anywhere, anywhere, anywhere],
        out_specs=(anywhere, anywhere),
        scratch_shapes=[
            vmem((FUNCS, ROWS, LANES)),
            vmem((FUNCS, ROWS, LANES)),
            vmem((FUNCS, ROWS, LANES)),
            vmem((FUNCS, ROWS, LANES)),
            vmem((ROWS, LANES), f32),
            vmem((ROWS, LANES), f32),
            vmem((len(mixes), ROWS, LANES)),
            vmem((FUNCS, ROWS, LANES), f32),
            vmem((NXC + 1, NZC, 2, TILES, TILE, LANES)),
            vmem(((FUNCS + 1) * PLANES, 8, LANES), f32),
            pltpu.SMEM((64,), jnp.int32),
            vmem((NZC, NXC, ROWS, LANES)),
            vmem((NZC, NXC, ROWS, LANES)),
            vmem((NZC, NXC, ROWS, LANES)),
            vmem((NZC, 2, HA, LANES)),
            vmem((NZC, 2, RA, LANES)),
            vmem((2, HA, LANES)),
            vmem((3, 2, RA, LANES)),
            vmem((2, NXC, HB, LANES)),
            vmem((3, 2, NXC, RB, LANES)),
            vmem((2, HB, LANES)),
            vmem((2, RB, LANES)),
            pltpu.SemaphoreType.DMA((4,)),
            pltpu.SemaphoreType.DMA((PAIRS + 1,)),
            pltpu.SemaphoreType.DMA((copies,)),
            pltpu.SemaphoreType.DMA((copies,)),
        ],
        compiler_params=pltpu.CompilerParams(
            collective_id=0, has_side_effects=True, vmem_limit_bytes=60 * 1024 * 1024
        ),
    )(
        corners,
        occupation.astype(f32),
        support.reshape(FUNCS, ROWS, LANES),
        potential.reshape(ROWS, LANES),
        jnp.asarray(mixes),
    )
    return applied.reshape(support.shape), density.reshape(potential.shape)


def solution(mesh):
    in_specs = (P("grp", None, "slab", None), P("grp"), P("grp"), P("grp", "slab", None))
    out_specs = (P("grp", None, "slab", None), P("grp", "slab", None))
    return jax.shard_map(
        on_device, mesh=mesh, in_specs=in_specs, out_specs=out_specs, check_vma=False
    )
```

time: 60 us -> 47.1 us (0.79)
  the two profiles are of different devices: /device:TPU:8 before, /device:TPU:1 now
where the time goes in v2:
time: 47.1 us; the launch traced here: 46.9 us
  Pallas kernels  42.1 us (89%)
  local copies, waits for them, and re-layouts  3.64 us (8%)
  between operations  0.66 us (1%)
  other arithmetic  0.51 us (1%)
    pallas_call x1, Pallas kernels, on_device(): pl.pallas_call(kernel, out_shape=(jax.ShapeDtypeStruct((FUNCS, ROWS, LANE...  42.1 us
    unnamed x6, local copies, waits for them, and re-layouts  3.64 us

profile of v2, /device:TPU:1, one launch (start us, length us, event | category | flops | bytes accessed | tf_op | source)
XLA Modules:
  0.0 46.9 jit_solution(11491696512300301365)
XLA Ops:
  0.6 0.0 copy-start.1
  0.6 0.6 %copy-done.1 = bf16[16]{0:T(256)(128)(2,1)S(1)} copy-done((bf16[16]{0:T(256)(128)(2,1)S(1)}, bf16[16]{0:T(256)(128)(2,1)}, u32[]{:S(2)}) %copy-start.1) | copy-done | bytes 56
  1.3 0.5 %convert_element_type.3.occupation = f32[16]{0:T(128)} convert(bf16[16]{0:T(256)(128)(2,1)S(1)} %copy-done.1) | non-fusion elementwise | flops 16 | bytes 96 | tf_op jit(solution)/shard_map/convert_element_type | solution.py:468
  1.8 42.1 %shard_map.68 = (bf16[16,256,128]{2,1,0:T(8,128)(2,1)}, f32[256,128]{1,0:T(8,128)}) custom-call(s32[16]{0:T(128)} %corners.1, f32[16]{0:T(128)} %convert_element_type.3.occupation, bf16[16,256,128]{2,1,0:T(8,128)(2,1)} %bitcast.4, f32[256,128]{1,0:T(8,128)} %bitcast.6, bf16[13,32,8,128]{3,2,1,0:T(8,128)(2,1)} %constant.2.clone.mixes_in), custom_call_target="tpu_custom_call" | custom-call | tf_op jit(solution)/shard_map/pallas_call | solution.py:427
  43.9 0.0 copy-start
  43.9 2.3 %copy.9 = bf16[16,32,8,128]{3,2,1,0:T(8,128)(2,1)} copy(bf16[16,32,8,128]{3,2,1,0:T(8,128)(2,1)} %bitcast.5) | data formatting | bytes 2097152
  46.3 0.0 copy-done
  46.3 0.7 %copy.10 = f32[32,8,128]{2,1,0:T(8,128)} copy(f32[32,8,128]{2,1,0:T(8,128)S(1)} %bitcast.7) | data formatting | bytes 262144
Async XLA Ops:
  0.6 0.7 %copy-start.1 = (bf16[16]{0:T(256)(128)(2,1)S(1)}, bf16[16]{0:T(256)(128)(2,1)}, u32[]{:S(2)}) copy-start(bf16[16]{0:T(256)(128)(2,1)} %param.7) | copy-start | bytes 100
  43.9 2.3 %copy-start = (f32[256,128]{1,0:T(8,128)S(1)}, f32[256,128]{1,0:T(8,128)}, u32[]{:S(2)}) copy-start(f32[256,128]{1,0:T(8,128)} %get-tuple-element.5) | copy-start | bytes 393220

commit v3 on v2

--- a/solution.py
+++ b/solution.py
@@ -18,6 +18,7 @@
 RA = 160
 RB = ROWS - RA
 HA, HB = RA // 2, RB // 2
+SENT_ROWS = 40448
 
 kinetic_taps = [
     2.0 * (-1.0) ** (index + 2) / float((index + 1) * (index + 1)) for index in range(8)
@@ -26,30 +27,30 @@
 
 
 ORDER = (
-    ("bx1",), ("az", 1, 0), ("az", 1, 1), ("bpart", 4), ("ax1", 0), ("halo",), ("bpart", 5), ("bx2", 0),
-    ("bx2", 1), ("bown", 4), ("rax1", 4), ("rbz", 2, 1), ("ax1", 7), ("az", 2, 1), ("bpart", 3), ("az", 2, 0),
-    ("rbz", 0, 1), ("rbz", 3, 1), ("bpart", 2), ("ax1", 1), ("bown", 5), ("rax1", 5), ("rbz", 1, 1),
-    ("bpart", 6), ("bown", 3), ("rax1", 3), ("bz", 1, 1), ("bz", 1, 0), ("ax2", 0, 0), ("ax2", 0, 1),
-    ("rbz", 2, 2, 0), ("rax2", 4, 1), ("rax2", 4, 0), ("bown", 2), ("bpart", 7), ("rax1", 2),
-    ("rbz", 2, 2, 1), ("bown", 6), ("bpart", 0), ("az", 3, 1), ("az", 3, 0), ("rax1", 6), ("ax1", 6),
-    ("bpart", 1), ("ax2", 1, 0), ("rbz", 1, 2, 0), ("rax2", 3, 1), ("rbz", 3, 2, 0), ("rbz", 3, 2, 1),
-    ("rax2", 3, 0), ("rbz", 1, 2, 1), ("rbz", 0, 2, 0), ("ax2", 1, 1), ("bown", 0), ("rax2", 5, 0),
-    ("ax1", 2), ("rax2", 5, 1), ("ax2", 7, 1), ("rbz", 0, 2, 1), ("bown", 7), ("rax1", 7), ("rax3", 4),
-    ("raz", 1), ("rbz", 2, 3, 0), ("rbz", 2, 3, 1), ("rax2", 2, 1), ("rax2", 6, 0), ("bz", 2, 1),
-    ("bz", 2, 0), ("bown", 1), ("rax1", 1), ("lap", 2), ("rbz", 1, 3, 1), ("rax3", 3), ("rax2", 2, 0),
-    ("az", 4, 0), ("ax2", 6, 0), ("az", 4, 1), ("raz", 2, 0), ("rax2", 6, 1), ("rbz", 1, 3, 0),
-    ("rbz", 2, 4, 1), ("lap", 0), ("ax1", 5), ("rbz", 2, 4, 0), ("rbz", 3, 3, 0), ("ax2", 6, 1),
-    ("rbz", 3, 3, 1), ("lap", 3), ("rax3", 5), ("ax2", 2, 1), ("raz", 2, 1), ("ax1", 3), ("bz", 3, 1),
-    ("ax2", 7, 0), ("rbz", 0, 3, 1), ("bp", 0), ("bz", 3, 0), ("rax2", 7, 0), ("bp", 2, 0), ("ax1", 4),
-    ("rbz", 1, 4, 1), ("rax1", 0), ("rbz", 0, 3, 0), ("rax2", 1, 0), ("ap", 1), ("ax2", 2, 0), ("rax2", 7, 1),
-    ("rax3", 2), ("raz", 3, 0), ("rax3", 6), ("raz", 3, 1), ("rbz", 1, 4, 0), ("rbz", 3, 4, 0),
-    ("rax2", 1, 1), ("rbx1",), ("bp", 1, 0), ("ax2", 5, 0), ("ax2", 5, 1), ("rbz", 3, 4, 1), ("lap", 1),
-    ("ax2", 3, 0), ("bp", 3, 0), ("ax2", 3, 1), ("bz", 4, 0), ("bz", 4, 1), ("ax2", 4, 0), ("ap", 0),
-    ("ax2", 4, 1), ("bp", 2, 1), ("ap", 6), ("rbz", 0, 4, 0), ("rbz", 0, 4, 1), ("rax2", 0, 1),
-    ("rax2", 0, 0), ("rax3", 7), ("raz", 4, 1), ("ap", 7), ("ap", 2), ("rax3", 1), ("raz", 4, 0), ("rbx2", 1),
-    ("bp", 1, 1), ("rbx2", 0), ("ap", 5), ("lap", 4), ("bp", 3, 1), ("ap", 3), ("ap", 4), ("bp", 4),
-    ("lap", 5), ("rax3", 0), ("lap", 6), ("lap", 7), ("agend",), ("fin", 6), ("fin", 0), ("fin", 3),
-    ("fin", 2), ("fin", 1), ("fin", 7), ("fin", 4), ("fin", 5), ("rsend",),
+    ("az", 1, 1), ("bx1",), ("az", 1, 0), ("bpart", 4), ("ax1", 0), ("bpart", 5), ("halo",), ("bpart", 3),
+    ("bown", 4), ("rax1", 4), ("rbz", 1, 1), ("bown", 5), ("rax1", 5), ("rbz", 2, 1), ("bx2", 0), ("bx2", 1),
+    ("ax1", 1), ("az", 2, 0), ("az", 2, 1), ("bown", 3), ("rax1", 3), ("rbz", 0, 1), ("bpart", 6), ("ax1", 7),
+    ("ax2", 0, 1), ("bpart", 2), ("rbz", 3, 1), ("rbz", 1, 2, 0), ("rbz", 1, 2, 1), ("rax2", 4, 0),
+    ("rax2", 4, 1), ("rbz", 2, 2, 1), ("rbz", 2, 2, 0), ("bz", 1, 1), ("bz", 1, 0), ("ax2", 0, 0),
+    ("bown", 2), ("rax1", 2), ("bown", 6), ("rax1", 6), ("rax2", 5, 1), ("az", 3, 0), ("rax2", 5, 0),
+    ("bpart", 7), ("rbz", 3, 2, 0), ("rbz", 3, 2, 1), ("rax2", 3, 1), ("rax2", 3, 0), ("az", 3, 1),
+    ("ax1", 6), ("rbz", 2, 3, 0), ("ax1", 2), ("rbz", 0, 2, 1), ("rax3", 4), ("raz", 1), ("bown", 7),
+    ("bpart", 1), ("rbz", 2, 3, 1), ("rbz", 0, 2, 0), ("rax2", 6, 1), ("rax1", 7), ("rax2", 6, 0),
+    ("rax2", 2, 0), ("bz", 2, 1), ("bz", 2, 0), ("rbz", 1, 3, 1), ("rax3", 5), ("bpart", 0), ("ax2", 1, 1),
+    ("ax2", 7, 1), ("az", 4, 0), ("ax2", 1, 0), ("az", 4, 1), ("bown", 1), ("rax2", 2, 1), ("rbz", 1, 3, 0),
+    ("rbz", 3, 3, 1), ("bown", 0), ("rax1", 0), ("rax1", 1), ("rbz", 2, 4, 0), ("rbz", 3, 3, 0),
+    ("rbz", 2, 4, 1), ("ax2", 7, 0), ("ap", 0), ("raz", 2, 1), ("ax2", 6, 1), ("ax2", 2, 1), ("ax1", 5),
+    ("ax2", 2, 0), ("rax3", 3), ("raz", 2, 0), ("ax1", 3), ("bz", 3, 1), ("bz", 3, 0), ("rax3", 6),
+    ("bp", 1, 1), ("lap", 2), ("ax1", 4), ("bp", 2, 1), ("rax2", 7, 1), ("ax2", 6, 0), ("lap", 0),
+    ("rbz", 0, 3, 1), ("rax2", 1, 1), ("rbz", 0, 3, 0), ("rbz", 3, 4, 1), ("rax2", 7, 0), ("lap", 3),
+    ("rbz", 1, 4, 0), ("ap", 1), ("raz", 3, 1), ("rax2", 1, 0), ("rax3", 2), ("raz", 3, 0), ("rbx1",),
+    ("rbz", 3, 4, 0), ("ax2", 5, 1), ("rbz", 1, 4, 1), ("ax2", 5, 0), ("ax2", 3, 0), ("ap", 7), ("ax2", 3, 1),
+    ("bz", 4, 1), ("bz", 4, 0), ("ax2", 4, 0), ("bp", 1, 0), ("ax2", 4, 1), ("rax2", 0, 1), ("rax2", 0, 0),
+    ("bp", 0), ("rbz", 0, 4, 1), ("lap", 5), ("bp", 3, 0), ("rbz", 0, 4, 0), ("ap", 2), ("ap", 6),
+    ("rax3", 7), ("bp", 3, 1), ("bp", 2, 0), ("raz", 4, 1), ("rax3", 1), ("raz", 4, 0), ("rbx2", 0),
+    ("rbx2", 1), ("ap", 5), ("ap", 3), ("lap", 1), ("ap", 4), ("bp", 4), ("lap", 4), ("lap", 6), ("rax3", 0),
+    ("lap", 7), ("agend",), ("fin", 1), ("fin", 5), ("fin", 0), ("fin", 4), ("fin", 3), ("fin", 2),
+    ("fin", 6), ("fin", 7), ("rsend",),
 )
 
 
@@ -87,11 +88,11 @@
 
 
 def kernel(
-    corners, occupation, support, potential, mixes_in,
+    corners_in, occupation_in, support, potential, mixes_in,
     applied, density,
-    own, left, right, out, pot_in, dens, mixes,
+    corners, occupation, weights, own, left, right, out, pot_in, dens, mixes,
     kinetic, gathered, terms, table, part_out, part_in, sums,
-    xa1, xa2, za1, za, zb1, zb, xb1, xb2,
+    xa1, xa2, za1, za, zb1, zb, xb1, xb2, tally,
     load_sem, out_sem, send_sem, recv_sem,
 ):
     f32, bf16 = jnp.float32, jnp.bfloat16
@@ -109,25 +110,26 @@
 
     loads = {}
     for index, (name, src, dst) in enumerate([
+        ("corners", corners_in, corners),
         ("potential", potential, pot_in),
+        ("occupation", occupation_in, occupation),
         ("support", support, own),
         ("mixes", mixes_in.reshape(mixes.shape), mixes),
     ]):
         loads[name] = pltpu.make_async_copy(src, dst, load_sem.at[index])
         loads[name].start()
 
-    sent, pending = {}, set()
+    slots, pending, rows = {}, {}, []
 
     def send(name, src, dst, device):
-        index = len(sent)
-        copy = pltpu.make_async_remote_copy(
+        index = slots.setdefault(name, len(slots))
+        rows.append(math.prod(src.shape[:-1]))
+        pending[name] = pending.get(name, 0) + rows[-1]
+        pltpu.make_async_remote_copy(
             src_ref=src, dst_ref=dst,
-            send_sem=send_sem.at[index], recv_sem=recv_sem.at[index],
+            send_sem=send_sem, recv_sem=recv_sem.at[index],
             device_id=device, device_id_type=MESH,
-        )
-        copy.start()
-        sent[name] = copy
-        pending.add(name)
+        ).start()
 
     barrier = pltpu.get_barrier_semaphore()
     neighbours = (*along_x, *along_z, *along_y, partner)
@@ -136,8 +138,8 @@
 
     def arrived(*name):
         if name in pending:
-            pending.remove(name)
-            sent[name].wait_recv()
+            whole = tally.at[pl.ds(0, pending.pop(name))]
+            pltpu.make_async_copy(whole, whole, recv_sem.at[slots[name]]).wait()
 
     def slot(dx, dz, start, size):
         tiles = pl.ds(start // TILE, size // TILE)
@@ -155,12 +157,11 @@
             arrived("az", step - 1, way)
         dz = from_way(way, step - 1)
         where = slot(0, dz, 0, RA) if step < 4 else slot(0, dz, way * HA, HA)
-        send(("az", step, way), where, where, along_z[way])
+        send(("az", 4) if step == 4 else ("az", step, way), where, where, along_z[way])
 
     def ax1(dz):
         if dz == 4:
-            arrived("az", 4, 0)
-            arrived("az", 4, 1)
+            arrived("az", 4)
         elif dz:
             arrived("az", min(dz, NZC - dz), 0 if dz > 4 else 1)
         for way in range(2):
@@ -170,13 +171,12 @@
     def ax2(dz, way):
         arrived("ax1", dz, way)
         where = slot(3 if way == 0 else 1, dz, way * HA, HA)
-        send(("ax2", dz, way), where, where, along_x[way])
+        send(("ax2", dz), where, where, along_x[way])
 
     def ap(dz):
-        for way in range(2):
-            arrived("ax2", dz, way)
+        arrived("ax2", dz)
         where = column(dz, 0, RA)
-        send(("ap", dz), where, where, partner)
+        send(("ap",), where, where, partner)
 
     def bx1():
         for way in range(2):
@@ -186,35 +186,30 @@
     def bx2(way):
         arrived("bx1", way)
         where = slot(3 if way == 0 else 1, 0, RA + way * HB, HB)
-        send(("bx2", way), where, where, along_x[way])
+        send(("bx2",), where, where, along_x[way])
 
     def bz(step, way):
         if step == 1:
-            arrived("bx2", 0)
-            arrived("bx2", 1)
+            arrived("bx2")
         else:
             arrived("bz", step - 1, way)
         dz = from_way(way, step - 1)
         where = column(dz, RA, RB) if step < 4 else column(dz, RA + way * HB, HB)
-        send(("bz", step, way), where, where, along_z[way])
+        send(("bz", 4) if step == 4 else ("bz", step, way), where, where, along_z[way])
 
     def bp(distance, way=0):
         if distance == 0:
-            arrived("bx2", 0)
-            arrived("bx2", 1)
+            arrived("bx2")
         elif distance == 4:
-            arrived("bz", 4, 0)
-            arrived("bz", 4, 1)
+            arrived("bz", 4)
         else:
             arrived("bz", distance, way)
         dz = from_way(way, distance)
         where = column(dz, RA, RB)
-        send(("bp", dz), where, where, partner)
+        send(("ap",), where, where, partner)
 
     def agend():
-        for dz in range(NZC):
-            arrived("ap", dz)
-            arrived("bp", dz)
+        arrived("ap")
         gathered[4, 0, 0] = gathered[0, 0, 0]
 
     def build(target, dz, owner, added=None):
@@ -262,11 +257,10 @@
         arrived("rax1", dz, way)
         add(sums.at[dz, dx], way * HA, HA, xa1.at[dz, way])
         part = sums.at[dz, dx, pl.ds(0, RA)]
-        send(("rax2", dz, way), part, xa2.at[dz, way], along_x[way])
+        send(("rax2", dz), part, xa2.at[dz, way], along_x[way])
 
     def rax3(dz):
-        for way in range(2):
-            arrived("rax2", dz, way)
+        arrived("rax2", dz)
         add(sums.at[dz, 0], 0, RA, xa2.at[dz, 0], xa2.at[dz, 1])
 
     def raz(step, way=None):
@@ -282,7 +276,7 @@
         else:
             add(sums.at[dz, 0], 0, RA, za.at[step - 3, way])
         part = sums.at[dz, 0, pl.ds(0, RA)]
-        send(("raz", step, way), part, za.at[step - 2, way], along_z[way])
+        send(("raz", 4) if step == 4 else ("raz", step, way), part, za.at[step - 2, way], along_z[way])
 
     def rbz(dx, step, way=None):
         if step == 1:
@@ -297,11 +291,10 @@
         else:
             add(sums.at[dz, dx], RA, RB, zb.at[step - 3, way, dx])
         part = sums.at[dz, dx, pl.ds(RA, RB)]
-        send(("rbz", dx, step, way), part, zb.at[step - 2, way, dx], along_z[way])
+        send(("rbz", dx, 4) if step == 4 else ("rbz", dx, step, way), part, zb.at[step - 2, way, dx], along_z[way])
 
     def rbz_end(dx):
-        for way in range(2):
-            arrived("rbz", dx, 4, way)
+        arrived("rbz", dx, 4)
         add(sums.at[0, dx], RA, RB, zb.at[2, 0, dx], zb.at[2, 1, dx])
 
     def rbx1():
@@ -315,14 +308,12 @@
         rbz_end(dx)
         arrived("rbx1", way)
         add(sums.at[0, dx], RA + way * HB, HB, xb1.at[way])
-        send(("rbx2", way), sums.at[0, dx, pl.ds(RA, RB)], xb2.at[way], along_x[way])
+        send(("rbx2",), sums.at[0, dx, pl.ds(RA, RB)], xb2.at[way], along_x[way])
 
     def rsend():
-        for way in range(2):
-            arrived("raz", 4, way)
-            for dx in range(NXC):
-                arrived("rbz", dx, 4, way)
-            arrived("rbx2", way)
+        arrived("raz", 4)
+        arrived("rbz", 0, 4)
+        arrived("rbx2")
         dens[pl.ds(0, RA), :] = (
             sums[0, 0, pl.ds(0, RA), :].astype(f32)
             + za[2, 0].astype(f32) + za[2, 1].astype(f32)
@@ -338,14 +329,13 @@
     def halo():
         for pair in range(PAIRS):
             where = pl.ds(2 * pair, 2)
-            send(("halo", pair, 0), support.at[where], left.at[where], y_next)
-            send(("halo", pair, 1), support.at[where], right.at[where], y_prev)
+            send(("halo", pair), support.at[where], left.at[where], y_next)
+            send(("halo", pair), support.at[where], right.at[where], y_prev)
 
     def lap(pair):
         if pair == first_lap:
             loads["mixes"].wait()
-        arrived("halo", pair, 0)
-        arrived("halo", pair, 1)
+        arrived("halo", pair)
         first = 2 * pair
         cells = jnp.concatenate([
             jnp.concatenate([ref[first], ref[first + 1]], axis=1) for ref in (own, left, right)
@@ -376,6 +366,7 @@
         )
         loads["out", pair].start()
 
+    loads["corners"].wait()
     bases = [corners[k] // 32 for k in range(FUNCS)]
 
     def find(block, carry):
@@ -389,18 +380,26 @@
     terms[pl.ds(FUNCS * PLANES, PLANES)] = jnp.zeros((PLANES, 8, LANES), f32)
     loads["potential"].wait()
     gathered[x, z, core] = pot_in[...].astype(bf16).reshape(TILES, TILE, LANES)
+    loads["occupation"].wait()
     loads["support"].wait()
+    spread = jnp.broadcast_to(occupation[...].astype(f32).reshape(1, FUNCS), (FUNCS, FUNCS))
+    lane = lax.broadcasted_iota(jnp.int32, (FUNCS, FUNCS), 1)
+    diagonal = lane == lax.broadcasted_iota(jnp.int32, (FUNCS, FUNCS), 0)
+    column_weights = jnp.sum(jnp.where(diagonal, spread, 0.0), axis=1, keepdims=True)
     for k in range(FUNCS):
-        value = own[k].astype(f32)
-        twin = k
-        for other in reversed(range(k + 1, FUNCS)):
-            twin = jnp.where(bases[other] == bases[k], other, twin)
-        total = occupation[k] * value * value
+        weights[k] = jnp.broadcast_to(column_weights[k:k + 1], (8, LANES))
+    weights[FUNCS] = jnp.zeros((8, LANES), f32)
+
+    for k in range(FUNCS):
+        value = own[k].astype(f32).reshape(PLANES, 8, LANES)
+        total = weights[k] * value * value
         if k + 1 < FUNCS:
-            second = own[twin].astype(f32)
-            weight = jnp.where(twin == k, 0.0, occupation[twin])
-            total = total + weight * second * second
-        terms[pl.ds(k * PLANES, PLANES)] = total.reshape(PLANES, 8, LANES)
+            twin = FUNCS
+            for other in reversed(range(k + 1, FUNCS)):
+                twin = jnp.where(bases[other] == bases[k], other, twin)
+            second = own[jnp.minimum(twin, FUNCS - 1)].astype(f32).reshape(PLANES, 8, LANES)
+            total = total + weights[twin] * second * second
+        terms[pl.ds(k * PLANES, PLANES)] = total
     pl.semaphore_wait(barrier, len(neighbours))
 
     steps = {step.__name__: step for step in (
@@ -410,29 +409,43 @@
     first_lap = next(args[0] for name, *args in ORDER if name == "lap")
     for name, *args in ORDER:
         steps[name](*args)
-    for copy in sent.values():
-        copy.wait_send()
+    assert sum(rows) == SENT_ROWS, sum(rows)
+    pltpu.make_async_copy(tally, tally, send_sem).wait()
     for pair in range(PAIRS):
         loads["out", pair].wait()
     loads["density"].wait()
+
+
+def store(applied, density, applied_out, density_out, sems):
+    copies = [
+        pltpu.make_async_copy(applied, applied_out, sems.at[0]),
+        pltpu.make_async_copy(density, density_out, sems.at[1]),
+    ]
+    for copy in copies:
+        copy.start()
+    for copy in copies:
+        copy.wait()
 
 
 def on_device(support, corners, occupation, potential):
     mixes = stencil_matrices()
     bf16, f32 = jnp.bfloat16, jnp.float32
     vmem = lambda shape, kind=bf16: pltpu.VMEM(shape, kind)
-    smem = pl.BlockSpec(memory_space=pltpu.SMEM)
+    in_hbm = lambda array: pltpu.with_memory_space_constraint(array, pltpu.HBM)
     anywhere = pl.BlockSpec(memory_space=pl.ANY)
-    copies = 192
+    copies = 122
     applied, density = pl.pallas_call(
         kernel,
         out_shape=(
             jax.ShapeDtypeStruct((FUNCS, ROWS, LANES), bf16),
             jax.ShapeDtypeStruct((ROWS, LANES), f32),
         ),
-        in_specs=[smem, smem, anywhere, anywhere, anywhere],
+        in_specs=[anywhere] * 5,
         out_specs=(anywhere, anywhere),
         scratch_shapes=[
+            pltpu.SMEM((FUNCS,), jnp.int32),
+            vmem((FUNCS,)),
+            vmem((FUNCS + 1, 8, LANES), f32),
             vmem((FUNCS, ROWS, LANES)),
             vmem((FUNCS, ROWS, LANES)),
             vmem((FUNCS, ROWS, LANES)),
@@ -455,21 +468,33 @@
             vmem((3, 2, NXC, RB, LANES)),
             vmem((2, HB, LANES)),
             vmem((2, RB, LANES)),
-            pltpu.SemaphoreType.DMA((4,)),
+            vmem((SENT_ROWS, LANES)),
+            pltpu.SemaphoreType.DMA((5,)),
             pltpu.SemaphoreType.DMA((PAIRS + 1,)),
-            pltpu.SemaphoreType.DMA((copies,)),
+            pltpu.SemaphoreType.DMA,
             pltpu.SemaphoreType.DMA((copies,)),
         ],
         compiler_params=pltpu.CompilerParams(
-            collective_id=0, has_side_effects=True, vmem_limit_bytes=60 * 1024 * 1024
+            collective_id=0, has_side_effects=True, vmem_limit_bytes=48 * 1024 * 1024
         ),
     )(
-        corners,
-        occupation.astype(f32),
-        support.reshape(FUNCS, ROWS, LANES),
-        potential.reshape(ROWS, LANES),
-        jnp.asarray(mixes),
+        in_hbm(corners),
+        in_hbm(occupation),
+        in_hbm(support.reshape(FUNCS, ROWS, LANES)),
+        in_hbm(potential.reshape(ROWS, LANES)),
+        in_hbm(jnp.asarray(mixes)),
     )
+    applied, density = pl.pallas_call(
+        store,
+        out_shape=(
+            jax.ShapeDtypeStruct((FUNCS, ROWS, LANES), bf16),
+            jax.ShapeDtypeStruct((ROWS, LANES), f32),
+        ),
+        in_specs=[anywhere] * 2,
+        out_specs=(anywhere, anywhere),
+        scratch_shapes=[pltpu.SemaphoreType.DMA((2,))],
+        compiler_params=pltpu.CompilerParams(vmem_limit_bytes=8 * 1024 * 1024),
+    )(applied, density)
     return applied.reshape(support.shape), density.reshape(potential.shape)
 
 

time: 47.1 us -> 41 us (0.87)
  local copies, waits for them, and re-layouts: 3.64 us -> 0 us
  Pallas kernels: 42.1 us -> 40.3 us
  other arithmetic: 0.51 us -> 0 us
    unnamed x6 -> x0, local copies, waits for them, and re-layouts: 3.64 us -> none
    pallas_call x1, Pallas kernels: 42.1 us -> 39.2 us  [on_device(): pl.pallas_call(kernel, out_shape=(jax.ShapeDtypeStruct((FUNCS, ROWS, LANE...]
    pallas_call x0 -> x1, Pallas kernels: none -> 1.02 us  [on_device(): pl.pallas_call(store, out_shape=(jax.ShapeDtypeStruct((FUNCS, ROWS, LANES...]
    convert_element_type x1 -> x0, other arithmetic: 0.51 us -> none  [on_device(): occupation.astype(f32)]
where the time goes in v3:
time: 41 us; the launch traced here: 40.9 us
  Pallas kernels  40.3 us (98%)
  between operations  0.64 us (2%)
    pallas_call x1, Pallas kernels, on_device(): pl.pallas_call(kernel, out_shape=(jax.ShapeDtypeStruct((FUNCS, ROWS, LANE...  39.2 us
    pallas_call x1, Pallas kernels, on_device(): pl.pallas_call(store, out_shape=(jax.ShapeDtypeStruct((FUNCS, ROWS, LANES...  1.02 us

profile of v3, /device:TPU:1, one launch (start us, length us, event | category | flops | bytes accessed | tf_op | source)
XLA Modules:
  0.0 40.9 jit_solution(13558312244052574439)
XLA Ops:
  0.6 39.2 %shard_map.68 = (bf16[16,256,128]{2,1,0:T(8,128)(2,1)S(1)}, f32[256,128]{1,0:T(8,128)S(1)}) custom-call(s32[16]{0:T(128)} %corners_in.1, bf16[16]{0:T(256)(128)(2,1)} %occupation_in.1, bf16[16,256,128]{2,1,0:T(8,128)(2,1)} %bitcast.4, f32[256,128]{1,0:T(8,128)} %bitcast.5, bf16[13,32,8,128]{3,2,1,0:T(8,128)(2,1)} %constant.2.clone.mixes_in), custom_call_target="tpu_custom_call" | custom-call | tf_op jit(solution)/shard_map/pallas_call | solution.py:437
  39.9 1.0 %shard_map.69 = (bf16[16,256,128]{2,1,0:T(8,128)(2,1)}, f32[256,128]{1,0:T(8,128)}) custom-call(bf16[16,256,128]{2,1,0:T(8,128)(2,1)S(1)} %get-tuple-element.6.applied, f32[256,128]{1,0:T(8,128)S(1)} %get-tuple-element.7.density), custom_call_target="tpu_custom_call" | custom-call | tf_op jit(solution)/shard_map/pallas_call | solution.py:487

commit v4 on v3

--- a/solution.py
+++ b/solution.py
@@ -90,10 +90,10 @@
 def kernel(
     corners_in, occupation_in, support, potential, mixes_in,
     applied, density,
-    corners, occupation, weights, own, left, right, out, pot_in, dens, mixes,
+    corners, occupation, weights, own, left, right, pot_in, mixes,
     kinetic, gathered, terms, table, part_out, part_in, sums,
     xa1, xa2, za1, za, zb1, zb, xb1, xb2, tally,
-    load_sem, out_sem, send_sem, recv_sem,
+    load_sem, send_sem, recv_sem,
 ):
     f32, bf16 = jnp.float32, jnp.bfloat16
     group, slab = lax.axis_index("grp"), lax.axis_index("slab")
@@ -314,17 +314,15 @@
         arrived("raz", 4)
         arrived("rbz", 0, 4)
         arrived("rbx2")
-        dens[pl.ds(0, RA), :] = (
+        density[pl.ds(0, RA), :] = (
             sums[0, 0, pl.ds(0, RA), :].astype(f32)
             + za[2, 0].astype(f32) + za[2, 1].astype(f32)
         )
-        dens[pl.ds(RA, RB), :] = (
+        density[pl.ds(RA, RB), :] = (
             sums[0, 0, pl.ds(RA, RB), :].astype(f32)
             + zb[2, 0, 0].astype(f32) + zb[2, 1, 0].astype(f32)
             + xb2[0].astype(f32) + xb2[1].astype(f32)
         )
-        loads["density"] = pltpu.make_async_copy(dens, density, out_sem.at[PAIRS])
-        loads["density"].start()
 
     def halo():
         for pair in range(PAIRS):
@@ -360,11 +358,7 @@
             window = flat[pl.ds(corner // 2, TILES + 1)].astype(f32).reshape(ROWS + TILE, LANES)
             local = jnp.where(corner % 2 == 1, window[8:8 + ROWS], window[:ROWS])
             term = (local * own[func].astype(f32)).astype(bf16).astype(f32)
-            out[func] = (kinetic[func] + term).astype(bf16)
-        loads["out", pair] = pltpu.make_async_copy(
-            out.at[pl.ds(first, 2)], applied.at[pl.ds(first, 2)], out_sem.at[pair]
-        )
-        loads["out", pair].start()
+            applied[func] = (kinetic[func] + term).astype(bf16)
 
     loads["corners"].wait()
     bases = [corners[k] // 32 for k in range(FUNCS)]
@@ -411,9 +405,6 @@
         steps[name](*args)
     assert sum(rows) == SENT_ROWS, sum(rows)
     pltpu.make_async_copy(tally, tally, send_sem).wait()
-    for pair in range(PAIRS):
-        loads["out", pair].wait()
-    loads["density"].wait()
 
 
 def store(applied, density, applied_out, density_out, sems):
@@ -433,15 +424,16 @@
     vmem = lambda shape, kind=bf16: pltpu.VMEM(shape, kind)
     in_hbm = lambda array: pltpu.with_memory_space_constraint(array, pltpu.HBM)
     anywhere = pl.BlockSpec(memory_space=pl.ANY)
+    in_vmem = pl.BlockSpec(memory_space=pltpu.VMEM)
     copies = 122
     applied, density = pl.pallas_call(
         kernel,
         out_shape=(
-            jax.ShapeDtypeStruct((FUNCS, ROWS, LANES), bf16),
-            jax.ShapeDtypeStruct((ROWS, LANES), f32),
+            pltpu.VMEM((FUNCS, ROWS, LANES), bf16),
+            pltpu.VMEM((ROWS, LANES), f32),
         ),
         in_specs=[anywhere] * 5,
-        out_specs=(anywhere, anywhere),
+        out_specs=(in_vmem, in_vmem),
         scratch_shapes=[
             pltpu.SMEM((FUNCS,), jnp.int32),
             vmem((FUNCS,)),
@@ -449,8 +441,6 @@
             vmem((FUNCS, ROWS, LANES)),
             vmem((FUNCS, ROWS, LANES)),
             vmem((FUNCS, ROWS, LANES)),
-            vmem((FUNCS, ROWS, LANES)),
-            vmem((ROWS, LANES), f32),
             vmem((ROWS, LANES), f32),
             vmem((len(mixes), ROWS, LANES)),
             vmem((FUNCS, ROWS, LANES), f32),
@@ -470,7 +460,6 @@
             vmem((2, RB, LANES)),
             vmem((SENT_ROWS, LANES)),
             pltpu.SemaphoreType.DMA((5,)),
-            pltpu.SemaphoreType.DMA((PAIRS + 1,)),
             pltpu.SemaphoreType.DMA,
             pltpu.SemaphoreType.DMA((copies,)),
         ],

time: 41 us -> 39 us (0.951)
  Pallas kernels: 40.3 us -> 38.3 us
    pallas_call x1, Pallas kernels: 39.2 us -> 37.3 us  [on_device(): pl.pallas_call(kernel, out_shape=(pltpu.VMEM((FUNCS, ROWS, LANES), bf16),...]
where the time goes in v4:
time: 39 us; the launch traced here: 38.9 us
  Pallas kernels  38.3 us (98%)
  between operations  0.64 us (2%)
    pallas_call x1, Pallas kernels, on_device(): pl.pallas_call(kernel, out_shape=(pltpu.VMEM((FUNCS, ROWS, LANES), bf16),...  37.3 us
    pallas_call x1, Pallas kernels, on_device(): pl.pallas_call(store, out_shape=(jax.ShapeDtypeStruct((FUNCS, ROWS, LANES...  1.02 us

profile of v4, /device:TPU:1, one launch (start us, length us, event | category | flops | bytes accessed | tf_op | source)
XLA Modules:
  0.0 38.9 jit_solution(8729301814552071349)
XLA Ops:
  0.6 37.3 %shard_map.68 = (bf16[16,256,128]{2,1,0:T(8,128)(2,1)S(1)}, f32[256,128]{1,0:T(8,128)S(1)}) custom-call(s32[16]{0:T(128)} %corners_in.1, bf16[16]{0:T(256)(128)(2,1)} %occupation_in.1, bf16[16,256,128]{2,1,0:T(8,128)(2,1)} %bitcast.4, f32[256,128]{1,0:T(8,128)} %bitcast.5, bf16[13,32,8,128]{3,2,1,0:T(8,128)(2,1)} %constant.2.clone.mixes_in), custom_call_target="tpu_custom_call" | custom-call | tf_op jit(solution)/shard_map/pallas_call | solution.py:429
  37.9 1.0 %shard_map.69 = (bf16[16,256,128]{2,1,0:T(8,128)(2,1)}, f32[256,128]{1,0:T(8,128)}) custom-call(bf16[16,256,128]{2,1,0:T(8,128)(2,1)S(1)} %get-tuple-element.6.applied, f32[256,128]{1,0:T(8,128)S(1)} %get-tuple-element.7.density), custom_call_target="tpu_custom_call" | custom-call | tf_op jit(solution)/shard_map/pallas_call | solution.py:476

commit v5 on v4

--- a/solution.py
+++ b/solution.py
@@ -15,9 +15,8 @@
 PAIRS = FUNCS // 2
 TILE = 16
 PLANES, TILES = ROWS // 8, ROWS // TILE
-RA = 160
-RB = ROWS - RA
-HA, HB = RA // 2, RB // 2
+GA, SA = 144, 160
+GB, SB = ROWS - GA, ROWS - SA
 SENT_ROWS = 40448
 
 kinetic_taps = [
@@ -27,31 +26,40 @@
 
 
 ORDER = (
-    ("az", 1, 1), ("bx1",), ("az", 1, 0), ("bpart", 4), ("ax1", 0), ("bpart", 5), ("halo",), ("bpart", 3),
-    ("bown", 4), ("rax1", 4), ("rbz", 1, 1), ("bown", 5), ("rax1", 5), ("rbz", 2, 1), ("bx2", 0), ("bx2", 1),
-    ("ax1", 1), ("az", 2, 0), ("az", 2, 1), ("bown", 3), ("rax1", 3), ("rbz", 0, 1), ("bpart", 6), ("ax1", 7),
-    ("ax2", 0, 1), ("bpart", 2), ("rbz", 3, 1), ("rbz", 1, 2, 0), ("rbz", 1, 2, 1), ("rax2", 4, 0),
-    ("rax2", 4, 1), ("rbz", 2, 2, 1), ("rbz", 2, 2, 0), ("bz", 1, 1), ("bz", 1, 0), ("ax2", 0, 0),
-    ("bown", 2), ("rax1", 2), ("bown", 6), ("rax1", 6), ("rax2", 5, 1), ("az", 3, 0), ("rax2", 5, 0),
-    ("bpart", 7), ("rbz", 3, 2, 0), ("rbz", 3, 2, 1), ("rax2", 3, 1), ("rax2", 3, 0), ("az", 3, 1),
-    ("ax1", 6), ("rbz", 2, 3, 0), ("ax1", 2), ("rbz", 0, 2, 1), ("rax3", 4), ("raz", 1), ("bown", 7),
-    ("bpart", 1), ("rbz", 2, 3, 1), ("rbz", 0, 2, 0), ("rax2", 6, 1), ("rax1", 7), ("rax2", 6, 0),
-    ("rax2", 2, 0), ("bz", 2, 1), ("bz", 2, 0), ("rbz", 1, 3, 1), ("rax3", 5), ("bpart", 0), ("ax2", 1, 1),
-    ("ax2", 7, 1), ("az", 4, 0), ("ax2", 1, 0), ("az", 4, 1), ("bown", 1), ("rax2", 2, 1), ("rbz", 1, 3, 0),
-    ("rbz", 3, 3, 1), ("bown", 0), ("rax1", 0), ("rax1", 1), ("rbz", 2, 4, 0), ("rbz", 3, 3, 0),
-    ("rbz", 2, 4, 1), ("ax2", 7, 0), ("ap", 0), ("raz", 2, 1), ("ax2", 6, 1), ("ax2", 2, 1), ("ax1", 5),
-    ("ax2", 2, 0), ("rax3", 3), ("raz", 2, 0), ("ax1", 3), ("bz", 3, 1), ("bz", 3, 0), ("rax3", 6),
-    ("bp", 1, 1), ("lap", 2), ("ax1", 4), ("bp", 2, 1), ("rax2", 7, 1), ("ax2", 6, 0), ("lap", 0),
-    ("rbz", 0, 3, 1), ("rax2", 1, 1), ("rbz", 0, 3, 0), ("rbz", 3, 4, 1), ("rax2", 7, 0), ("lap", 3),
-    ("rbz", 1, 4, 0), ("ap", 1), ("raz", 3, 1), ("rax2", 1, 0), ("rax3", 2), ("raz", 3, 0), ("rbx1",),
-    ("rbz", 3, 4, 0), ("ax2", 5, 1), ("rbz", 1, 4, 1), ("ax2", 5, 0), ("ax2", 3, 0), ("ap", 7), ("ax2", 3, 1),
-    ("bz", 4, 1), ("bz", 4, 0), ("ax2", 4, 0), ("bp", 1, 0), ("ax2", 4, 1), ("rax2", 0, 1), ("rax2", 0, 0),
-    ("bp", 0), ("rbz", 0, 4, 1), ("lap", 5), ("bp", 3, 0), ("rbz", 0, 4, 0), ("ap", 2), ("ap", 6),
-    ("rax3", 7), ("bp", 3, 1), ("bp", 2, 0), ("raz", 4, 1), ("rax3", 1), ("raz", 4, 0), ("rbx2", 0),
-    ("rbx2", 1), ("ap", 5), ("ap", 3), ("lap", 1), ("ap", 4), ("bp", 4), ("lap", 4), ("lap", 6), ("rax3", 0),
-    ("lap", 7), ("agend",), ("fin", 1), ("fin", 5), ("fin", 0), ("fin", 4), ("fin", 3), ("fin", 2),
-    ("fin", 6), ("fin", 7), ("rsend",),
+    ("bx1",), ("az", 1, 1), ("bpart", 4), ("az", 1, 0), ("bpart", 3), ("halo",), ("bpart", 5), ("ax1", 0),
+    ("bz", 0, 1, 1), ("bz", 0, 1, 0), ("bown", 4), ("rbz", 3, 1), ("rax1", 4), ("rbz", 2, 1), ("bpart", 6),
+    ("rbz", 0, 1), ("bown", 3), ("rax1", 3), ("rbz", 1, 1), ("bown", 5), ("rax1", 5), ("bz", 3, 1, 0),
+    ("bz", 3, 1, 1), ("bx2", 1), ("bz", 1, 1, 0), ("bz", 1, 1, 1), ("bx2", 0), ("ax1", 1), ("bown", 6),
+    ("bpart", 7), ("bpart", 1), ("az", 2, 1), ("az", 2, 0), ("ax1", 7), ("rax1", 6), ("bpart", 2),
+    ("bz", 0, 2, 0), ("bz", 0, 2, 1), ("rbz", 2, 2, 0), ("rax2", 4, 1), ("rbz", 2, 2, 1), ("rax2", 4, 0),
+    ("rbz", 1, 2, 0), ("rax2", 3, 0), ("ax2", 0, 0), ("rbz", 3, 2, 1), ("rbz", 3, 2, 0), ("bown", 2),
+    ("rax1", 2), ("bz", 3, 2, 1), ("bz", 3, 2, 0), ("rax2", 3, 1), ("bz", 2, 1, 1), ("rax2", 5, 1),
+    ("ax2", 0, 1), ("bz", 2, 1, 0), ("az", 3, 0), ("rbz", 1, 2, 1), ("az", 3, 1), ("rax2", 5, 0),
+    ("rax2", 6, 0), ("ax2", 7, 1), ("rbz", 0, 2, 1), ("bown", 7), ("rax1", 7), ("rbz", 2, 3, 1),
+    ("bz", 1, 2, 0), ("rax2", 6, 1), ("rbz", 1, 3, 0), ("ax1", 6), ("ax1", 2), ("lap", 0), ("rbz", 2, 3, 0),
+    ("rax3", 4), ("raz", 1), ("rbz", 0, 2, 0), ("rbz", 3, 3, 0), ("bz", 1, 2, 1), ("bz", 2, 2, 1),
+    ("ax2", 1, 0), ("rbz", 3, 3, 1), ("ax1", 3), ("az", 4, 0), ("az", 4, 1), ("bown", 1), ("rax1", 1),
+    ("bz", 0, 3, 0), ("rax2", 2, 0), ("rbz", 1, 3, 1), ("ax1", 5), ("lap", 1), ("rbz", 2, 4, 1),
+    ("rax2", 7, 0), ("bz", 2, 2, 0), ("rbz", 2, 4, 0), ("rax3", 5), ("rax2", 2, 1), ("raz", 2, 1),
+    ("rax3", 3), ("raz", 2, 0), ("bz", 1, 3, 1), ("rax3", 6), ("ap", 0), ("rax2", 7, 1), ("bz", 3, 3, 0),
+    ("bpart", 0), ("bz", 3, 3, 1), ("bz", 2, 3, 1), ("bz", 0, 3, 1), ("bz", 1, 3, 0), ("rbz", 0, 3, 1),
+    ("ax1", 4), ("ax2", 3, 0), ("lap", 3), ("bp", 0), ("rbz", 3, 4, 0), ("bown", 0), ("bz", 2, 3, 0),
+    ("rax1", 0), ("ax2", 3, 1), ("rbz", 0, 3, 0), ("rbx1",), ("bp", 2, 0), ("rbz", 3, 4, 1), ("rax2", 1, 1),
+    ("ax2", 1, 1), ("rax2", 1, 0), ("raz", 3, 1), ("rax3", 2), ("raz", 3, 0), ("rbz", 1, 4, 1),
+    ("bz", 1, 4, 1), ("bp", 1, 0), ("ax2", 5, 1), ("ax2", 7, 0), ("ax2", 5, 0), ("lap", 4), ("bp", 2, 1),
+    ("rbz", 1, 4, 0), ("bp", 1, 1), ("bz", 0, 4, 0), ("ax2", 6, 1), ("ax2", 6, 0), ("bz", 2, 4, 1),
+    ("ax2", 2, 1), ("bz", 1, 4, 0), ("ax2", 2, 0), ("bz", 3, 4, 0), ("bz", 3, 4, 1), ("bp", 3, 1),
+    ("ax2", 4, 1), ("bz", 0, 4, 1), ("ax2", 4, 0), ("rax2", 0, 1), ("rax2", 0, 0), ("bp", 3, 0), ("ap", 3),
+    ("rbz", 0, 4, 1), ("bz", 2, 4, 0), ("rbz", 0, 4, 0), ("rbx2", 1), ("rax3", 1), ("rax3", 7), ("raz", 4, 1),
+    ("raz", 4, 0), ("ap", 1), ("lap", 5), ("ap", 7), ("ap", 5), ("rbx2", 0), ("ap", 6), ("ap", 2), ("ap", 4),
+    ("bp", 4), ("lap", 2), ("lap", 6), ("rax3", 0), ("lap", 7), ("agend",), ("fin", 5), ("fin", 7),
+    ("fin", 0), ("fin", 6), ("fin", 3), ("fin", 4), ("fin", 2), ("fin", 1), ("rsend",),
 )
+
+
+def half(way, start, size):
+    first = (size // TILE + 1) // 2 * TILE
+    return (start, first) if way == 0 else (start + first, size - first)
 
 
 def split_bf16(matrix):
@@ -108,6 +116,11 @@
     y_next, y_prev = (group, (slab + 1) % 4), (group, (slab + 3) % 4)
     along_x, along_z, along_y = (x_next, x_prev), (z_next, z_prev), (y_next, y_prev)
 
+    barrier = pltpu.get_barrier_semaphore()
+    neighbours = (*along_x, *along_z, *along_y, partner)
+    for device in neighbours:
+        pl.semaphore_signal(barrier, inc=1, device_id=device, device_id_type=MESH)
+
     loads = {}
     for index, (name, src, dst) in enumerate([
         ("corners", corners_in, corners),
@@ -131,11 +144,6 @@
             device_id=device, device_id_type=MESH,
         ).start()
 
-    barrier = pltpu.get_barrier_semaphore()
-    neighbours = (*along_x, *along_z, *along_y, partner)
-    for device in neighbours:
-        pl.semaphore_signal(barrier, inc=1, device_id=device, device_id_type=MESH)
-
     def arrived(*name):
         if name in pending:
             whole = tally.at[pl.ds(0, pending.pop(name))]
@@ -156,7 +164,7 @@
         if step > 1:
             arrived("az", step - 1, way)
         dz = from_way(way, step - 1)
-        where = slot(0, dz, 0, RA) if step < 4 else slot(0, dz, way * HA, HA)
+        where = slot(0, dz, *((0, GA) if step < 4 else half(way, 0, GA)))
         send(("az", 4) if step == 4 else ("az", step, way), where, where, along_z[way])
 
     def ax1(dz):
@@ -165,47 +173,53 @@
         elif dz:
             arrived("az", min(dz, NZC - dz), 0 if dz > 4 else 1)
         for way in range(2):
-            where = slot(0, dz, 0, RA)
+            where = slot(0, dz, 0, GA)
             send(("ax1", dz, way), where, where, along_x[way])
 
     def ax2(dz, way):
         arrived("ax1", dz, way)
-        where = slot(3 if way == 0 else 1, dz, way * HA, HA)
+        where = slot(3 if way == 0 else 1, dz, *half(way, 0, GA))
         send(("ax2", dz), where, where, along_x[way])
 
     def ap(dz):
         arrived("ax2", dz)
-        where = column(dz, 0, RA)
+        where = column(dz, 0, GA)
         send(("ap",), where, where, partner)
 
     def bx1():
         for way in range(2):
-            where = slot(0, 0, RA, RB)
+            where = slot(0, 0, GA, GB)
             send(("bx1", way), where, where, along_x[way])
 
     def bx2(way):
         arrived("bx1", way)
-        where = slot(3 if way == 0 else 1, 0, RA + way * HB, HB)
+        where = slot(3 if way == 0 else 1, 0, *half(way, GA, GB))
         send(("bx2",), where, where, along_x[way])
 
-    def bz(step, way):
-        if step == 1:
+    def bz(dx, step, way):
+        if step > 1:
+            arrived("bz", dx, step - 1, way)
+        elif dx == 2:
             arrived("bx2")
-        else:
-            arrived("bz", step - 1, way)
+        elif dx:
+            arrived("bx1", 0 if dx == 3 else 1)
         dz = from_way(way, step - 1)
-        where = column(dz, RA, RB) if step < 4 else column(dz, RA + way * HB, HB)
-        send(("bz", 4) if step == 4 else ("bz", step, way), where, where, along_z[way])
+        where = slot(dx, dz, *((GA, GB) if step < 4 else half(way, GA, GB)))
+        send(("bz", dx, 4) if step == 4 else ("bz", dx, step, way), where, where, along_z[way])
 
     def bp(distance, way=0):
         if distance == 0:
+            arrived("bx1", 0)
+            arrived("bx1", 1)
             arrived("bx2")
         elif distance == 4:
-            arrived("bz", 4)
+            for dx in range(NXC):
+                arrived("bz", dx, 4)
         else:
-            arrived("bz", distance, way)
+            for dx in range(NXC):
+                arrived("bz", dx, distance, way)
         dz = from_way(way, distance)
-        where = column(dz, RA, RB)
+        where = column(dz, GA, GB)
         send(("ap",), where, where, partner)
 
     def agend():
@@ -249,77 +263,85 @@
 
     def rax1(dz):
         for way in range(2):
-            part = sums.at[dz, 2, pl.ds(way * HA, HA)]
-            send(("rax1", dz, way), part, xa1.at[dz, way], along_x[way])
+            start, size = half(way, 0, SA)
+            part = sums.at[dz, 2, pl.ds(start, size)]
+            send(("rax1", dz, way), part, xa1.at[dz, way, pl.ds(0, size)], along_x[way])
 
     def rax2(dz, way):
         dx = 1 if way == 0 else 3
         arrived("rax1", dz, way)
-        add(sums.at[dz, dx], way * HA, HA, xa1.at[dz, way])
-        part = sums.at[dz, dx, pl.ds(0, RA)]
+        start, size = half(way, 0, SA)
+        add(sums.at[dz, dx], start, size, xa1.at[dz, way, pl.ds(0, size)])
+        part = sums.at[dz, dx, pl.ds(0, SA)]
         send(("rax2", dz), part, xa2.at[dz, way], along_x[way])
 
     def rax3(dz):
         arrived("rax2", dz)
-        add(sums.at[dz, 0], 0, RA, xa2.at[dz, 0], xa2.at[dz, 1])
+        add(sums.at[dz, 0], 0, SA, xa2.at[dz, 0], xa2.at[dz, 1])
 
     def raz(step, way=None):
         if step == 1:
             for way in range(2):
-                part = sums.at[4, 0, pl.ds(way * HA, HA)]
-                send(("raz", 1, way), part, za1.at[way], along_z[way])
+                start, size = half(way, 0, SA)
+                part = sums.at[4, 0, pl.ds(start, size)]
+                send(("raz", 1, way), part, za1.at[way, pl.ds(0, size)], along_z[way])
             return
         dz = 5 - step if way == 0 else 3 + step
         arrived("raz", step - 1, way)
         if step == 2:
-            add(sums.at[dz, 0], way * HA, HA, za1.at[way])
+            start, size = half(way, 0, SA)
+            add(sums.at[dz, 0], start, size, za1.at[way, pl.ds(0, size)])
         else:
-            add(sums.at[dz, 0], 0, RA, za.at[step - 3, way])
-        part = sums.at[dz, 0, pl.ds(0, RA)]
+            add(sums.at[dz, 0], 0, SA, za.at[step - 3, way])
+        part = sums.at[dz, 0, pl.ds(0, SA)]
         send(("raz", 4) if step == 4 else ("raz", step, way), part, za.at[step - 2, way], along_z[way])
 
     def rbz(dx, step, way=None):
         if step == 1:
             for way in range(2):
-                part = sums.at[4, dx, pl.ds(RA + way * HB, HB)]
-                send(("rbz", dx, 1, way), part, zb1.at[way, dx], along_z[way])
+                start, size = half(way, SA, SB)
+                part = sums.at[4, dx, pl.ds(start, size)]
+                send(("rbz", dx, 1, way), part, zb1.at[way, dx, pl.ds(0, size)], along_z[way])
             return
         dz = 5 - step if way == 0 else 3 + step
         arrived("rbz", dx, step - 1, way)
         if step == 2:
-            add(sums.at[dz, dx], RA + way * HB, HB, zb1.at[way, dx])
+            start, size = half(way, SA, SB)
+            add(sums.at[dz, dx], start, size, zb1.at[way, dx, pl.ds(0, size)])
         else:
-            add(sums.at[dz, dx], RA, RB, zb.at[step - 3, way, dx])
-        part = sums.at[dz, dx, pl.ds(RA, RB)]
+            add(sums.at[dz, dx], SA, SB, zb.at[step - 3, way, dx])
+        part = sums.at[dz, dx, pl.ds(SA, SB)]
         send(("rbz", dx, 4) if step == 4 else ("rbz", dx, step, way), part, zb.at[step - 2, way, dx], along_z[way])
 
     def rbz_end(dx):
         arrived("rbz", dx, 4)
-        add(sums.at[0, dx], RA, RB, zb.at[2, 0, dx], zb.at[2, 1, dx])
+        add(sums.at[0, dx], SA, SB, zb.at[2, 0, dx], zb.at[2, 1, dx])
 
     def rbx1():
         rbz_end(2)
         for way in range(2):
-            part = sums.at[0, 2, pl.ds(RA + way * HB, HB)]
-            send(("rbx1", way), part, xb1.at[way], along_x[way])
+            start, size = half(way, SA, SB)
+            part = sums.at[0, 2, pl.ds(start, size)]
+            send(("rbx1", way), part, xb1.at[way, pl.ds(0, size)], along_x[way])
 
     def rbx2(way):
         dx = 1 if way == 0 else 3
         rbz_end(dx)
         arrived("rbx1", way)
-        add(sums.at[0, dx], RA + way * HB, HB, xb1.at[way])
-        send(("rbx2",), sums.at[0, dx, pl.ds(RA, RB)], xb2.at[way], along_x[way])
+        start, size = half(way, SA, SB)
+        add(sums.at[0, dx], start, size, xb1.at[way, pl.ds(0, size)])
+        send(("rbx2",), sums.at[0, dx, pl.ds(SA, SB)], xb2.at[way], along_x[way])
 
     def rsend():
         arrived("raz", 4)
         arrived("rbz", 0, 4)
         arrived("rbx2")
-        density[pl.ds(0, RA), :] = (
-            sums[0, 0, pl.ds(0, RA), :].astype(f32)
+        density[pl.ds(0, SA), :] = (
+            sums[0, 0, pl.ds(0, SA), :].astype(f32)
             + za[2, 0].astype(f32) + za[2, 1].astype(f32)
         )
-        density[pl.ds(RA, RB), :] = (
-            sums[0, 0, pl.ds(RA, RB), :].astype(f32)
+        density[pl.ds(SA, SB), :] = (
+            sums[0, 0, pl.ds(SA, SB), :].astype(f32)
             + zb[2, 0, 0].astype(f32) + zb[2, 1, 0].astype(f32)
             + xb2[0].astype(f32) + xb2[1].astype(f32)
         )
@@ -425,7 +447,7 @@
     in_hbm = lambda array: pltpu.with_memory_space_constraint(array, pltpu.HBM)
     anywhere = pl.BlockSpec(memory_space=pl.ANY)
     in_vmem = pl.BlockSpec(memory_space=pltpu.VMEM)
-    copies = 122
+    copies = 144
     applied, density = pl.pallas_call(
         kernel,
         out_shape=(
@@ -450,14 +472,14 @@
             vmem((NZC, NXC, ROWS, LANES)),
             vmem((NZC, NXC, ROWS, LANES)),
             vmem((NZC, NXC, ROWS, LANES)),
-            vmem((NZC, 2, HA, LANES)),
-            vmem((NZC, 2, RA, LANES)),
-            vmem((2, HA, LANES)),
-            vmem((3, 2, RA, LANES)),
-            vmem((2, NXC, HB, LANES)),
-            vmem((3, 2, NXC, RB, LANES)),
-            vmem((2, HB, LANES)),
-            vmem((2, RB, LANES)),
+            vmem((NZC, 2, half(0, 0, SA)[1], LANES)),
+            vmem((NZC, 2, SA, LANES)),
+            vmem((2, half(0, 0, SA)[1], LANES)),
+            vmem((3, 2, SA, LANES)),
+            vmem((2, NXC, half(0, 0, SB)[1], LANES)),
+            vmem((3, 2, NXC, SB, LANES)),
+            vmem((2, half(0, 0, SB)[1], LANES)),
+            vmem((2, SB, LANES)),
             vmem((SENT_ROWS, LANES)),
             pltpu.SemaphoreType.DMA((5,)),
             pltpu.SemaphoreType.DMA,

time: 39 us -> 38.9 us (level)
  no operation moved by 1% of the time
where the time goes in v5:
time: 38.9 us
  Pallas kernels  38.2 us (98%)
  between operations  0.64 us (2%)
    pallas_call x1, Pallas kernels, on_device(): pl.pallas_call(kernel, out_shape=(pltpu.VMEM((FUNCS, ROWS, LANES), bf16),...  37.2 us
    pallas_call x1, Pallas kernels, on_device(): pl.pallas_call(store, out_shape=(jax.ShapeDtypeStruct((FUNCS, ROWS, LANES...  1.02 us

profile of v5, /device:TPU:1, one launch (start us, length us, event | category | flops | bytes accessed | tf_op | source)
XLA Modules:
  0.0 38.9 jit_solution(14413985607952531132)
XLA Ops:
  0.6 37.2 %shard_map.68 = (bf16[16,256,128]{2,1,0:T(8,128)(2,1)S(1)}, f32[256,128]{1,0:T(8,128)S(1)}) custom-call(s32[16]{0:T(128)} %corners_in.1, bf16[16]{0:T(256)(128)(2,1)} %occupation_in.1, bf16[16,256,128]{2,1,0:T(8,128)(2,1)} %bitcast.4, f32[256,128]{1,0:T(8,128)} %bitcast.5, bf16[13,32,8,128]{3,2,1,0:T(8,128)(2,1)} %constant.2.clone.mixes_in), custom_call_target="tpu_custom_call" | custom-call | tf_op jit(solution)/shard_map/pallas_call | solution.py:451
  37.8 1.0 %shard_map.69 = (bf16[16,256,128]{2,1,0:T(8,128)(2,1)}, f32[256,128]{1,0:T(8,128)}) custom-call(bf16[16,256,128]{2,1,0:T(8,128)(2,1)S(1)} %get-tuple-element.6.applied, f32[256,128]{1,0:T(8,128)S(1)} %get-tuple-element.7.density), custom_call_target="tpu_custom_call" | custom-call | tf_op jit(solution)/shard_map/pallas_call | solution.py:498

commit v6 on v4

--- a/solution.py
+++ b/solution.py
@@ -18,6 +18,8 @@
 RA = 160
 RB = ROWS - RA
 HA, HB = RA // 2, RB // 2
+EARLY = (4, 5, 3,)
+STORES = 4
 SENT_ROWS = 40448
 
 kinetic_taps = [
@@ -108,6 +110,11 @@
     y_next, y_prev = (group, (slab + 1) % 4), (group, (slab + 3) % 4)
     along_x, along_z, along_y = (x_next, x_prev), (z_next, z_prev), (y_next, y_prev)
 
+    barrier = pltpu.get_barrier_semaphore()
+    neighbours = (*along_x, *along_z, *along_y, partner)
+    for device in neighbours:
+        pl.semaphore_signal(barrier, inc=1, device_id=device, device_id_type=MESH)
+
     loads = {}
     for index, (name, src, dst) in enumerate([
         ("corners", corners_in, corners),
@@ -130,11 +137,6 @@
             send_sem=send_sem, recv_sem=recv_sem.at[index],
             device_id=device, device_id_type=MESH,
         ).start()
-
-    barrier = pltpu.get_barrier_semaphore()
-    neighbours = (*along_x, *along_z, *along_y, partner)
-    for device in neighbours:
-        pl.semaphore_signal(barrier, inc=1, device_id=device, device_id_type=MESH)
 
     def arrived(*name):
         if name in pending:
@@ -234,7 +236,8 @@
         lax.fori_loop(0, NXC, one, 0)
 
     def bpart(dz):
-        build(part_out, dz, 1 - core)
+        if dz not in EARLY:
+            build(part_out, dz, 1 - core)
         send(("part", dz), part_out.at[dz], part_in.at[dz], partner)
 
     def bown(dz):
@@ -394,6 +397,8 @@
             second = own[jnp.minimum(twin, FUNCS - 1)].astype(f32).reshape(PLANES, 8, LANES)
             total = total + weights[twin] * second * second
         terms[pl.ds(k * PLANES, PLANES)] = total
+    for dz in EARLY:
+        build(part_out, dz, 1 - core)
     pl.semaphore_wait(barrier, len(neighbours))
 
     steps = {step.__name__: step for step in (
@@ -408,10 +413,12 @@
 
 
 def store(applied, density, applied_out, density_out, sems):
-    copies = [
-        pltpu.make_async_copy(applied, applied_out, sems.at[0]),
-        pltpu.make_async_copy(density, density_out, sems.at[1]),
-    ]
+    copies = [pltpu.make_async_copy(density, density_out, sems.at[STORES])]
+    for piece in range(STORES):
+        where = pl.ds(piece * FUNCS // STORES, FUNCS // STORES)
+        copies.append(
+            pltpu.make_async_copy(applied.at[where], applied_out.at[where], sems.at[piece])
+        )
     for copy in copies:
         copy.start()
     for copy in copies:
@@ -481,7 +488,7 @@
         ),
         in_specs=[anywhere] * 2,
         out_specs=(anywhere, anywhere),
-        scratch_shapes=[pltpu.SemaphoreType.DMA((2,))],
+        scratch_shapes=[pltpu.SemaphoreType.DMA((STORES + 1,))],
         compiler_params=pltpu.CompilerParams(vmem_limit_bytes=8 * 1024 * 1024),
     )(applied, density)
     return applied.reshape(support.shape), density.reshape(potential.shape)

time: 39 us -> 39 us (level)
  no operation moved by 1% of the time
where the time goes in v6:
time: 39 us; the launch traced here: 38.9 us
  Pallas kernels  38.3 us (98%)
  between operations  0.64 us (2%)
    pallas_call x1, Pallas kernels, on_device(): pl.pallas_call(kernel, out_shape=(pltpu.VMEM((FUNCS, ROWS, LANES), bf16),...  37.2 us
    pallas_call x1, Pallas kernels, on_device(): pl.pallas_call(store, out_shape=(jax.ShapeDtypeStruct((FUNCS, ROWS, LANES...  1.05 us

profile of v6, /device:TPU:1, one launch (start us, length us, event | category | flops | bytes accessed | tf_op | source)
XLA Modules:
  0.0 38.9 jit_solution(10665826142429150347)
XLA Ops:
  0.6 37.2 %shard_map.68 = (bf16[16,256,128]{2,1,0:T(8,128)(2,1)S(1)}, f32[256,128]{1,0:T(8,128)S(1)}) custom-call(s32[16]{0:T(128)} %corners_in.1, bf16[16]{0:T(256)(128)(2,1)} %occupation_in.1, bf16[16,256,128]{2,1,0:T(8,128)(2,1)} %bitcast.4, f32[256,128]{1,0:T(8,128)} %bitcast.5, bf16[13,32,8,128]{3,2,1,0:T(8,128)(2,1)} %constant.2.clone.mixes_in), custom_call_target="tpu_custom_call" | custom-call | tf_op jit(solution)/shard_map/pallas_call | solution.py:436
  37.9 1.0 %shard_map.69 = (bf16[16,256,128]{2,1,0:T(8,128)(2,1)}, f32[256,128]{1,0:T(8,128)}) custom-call(bf16[16,256,128]{2,1,0:T(8,128)(2,1)S(1)} %get-tuple-element.6.applied, f32[256,128]{1,0:T(8,128)S(1)} %get-tuple-element.7.density), custom_call_target="tpu_custom_call" | custom-call | tf_op jit(solution)/shard_map/pallas_call | solution.py:483
